TPU v7x, 128 devices: a whole 4x4x4 slice. The times are simulated.
128 devices in a mesh: seq: 32 (over y, x, core), frm: 4 (over z).
Axes of the slice: x: 4, y: 4, z: 4, core: 2. Of those that a mesh axis runs over, the one named last changes fastest.
Arguments:
- hidden_in: bfloat16 [4, 4096, 5120], P('frm', 'seq'), may hold values from -6 to 6
- shift_mod: float32 [5120], replicated, may hold values from -3 to 3
- scale_mod: float32 [5120], replicated, may hold values from -3 to 3
- gate_mod: float32 [5120], replicated, may hold values from 1 to 3
- w_qkv: bfloat16 [5120, 12, 6, 128], P(None, 'frm'), may hold values from -0.078125 to 0.078125
- norm_gain: float32 [12, 4, 128], P('frm'), may hold values from 1.2 to 2.4
- w_out: bfloat16 [12, 2, 128, 5120], P('frm', None, None, 'seq'), may hold values from -0.109375 to 0.109375
- spatial_mask: int32 [12, 4, 32, 32], P('frm'), may hold values from 0 to 1, as said below
- temporal_mask: int32 [12, 32, 4, 4], P('frm'), may hold values from 0 to 1, as said below
- frame_order: int32 [4], replicated, may hold values from 0 to 3, each once
Outputs:
- layer_out: bfloat16 [4, 4096, 5120], P('frm', 'seq')
Inputs may be any that keep to these rules, and one draw needn't show every extreme that they name: `spatial_mask`: every block on the diagonal (query block equal to key block) is 1. `temporal_mask`: every entry with the query frame equal to the key frame is 1.
All inputs are finite; a program needn't handle non-finite values.
Results may differ from a plain program's by a relative error of at most 0.018.
Values may be sent and summed in bfloat16 or wider, within the bound.
No kernel may reach another device: no remote copies, remote signals or barrier semaphores. Data moves between devices by JAX's collectives and lax.ppermute only.
A program may use at most 192 MiB of HBM per device.

v0:
```python
import math

import jax
import jax.numpy as jnp
from jax import lax
from jax.experimental import pallas as pl
from jax.experimental.pallas import tpu as pltpu
from jax.sharding import Mesh, PartitionSpec as P

HP = 12
BLK = 128
HD = 128
EPS = 1e-06
LOG2E = 1.4426950408889634
OFF = -1e30
REL = (0, 2, 1, -1)
VMEM = 30 * 1024 * 1024
WIDE, NARROW = 40 * 1024 * 1024, 16 * 1024 * 1024


def params(limit=VMEM):
    return pltpu.CompilerParams(vmem_limit_bytes=limit)


def whole():
    return pl.BlockSpec(memory_space=pltpu.VMEM)


def cost(flops, size, trans=0):
    return pl.CostEstimate(flops=int(flops), bytes_accessed=int(size), transcendentals=int(trans))


def modulate_kernel(hidden_ref, shift_ref, scale_ref, low_ref, high_ref):
    rows = low_ref.shape[0]
    for at, out_ref in ((0, low_ref), (rows, high_ref)):
        values = hidden_ref[at : at + rows].astype(jnp.float32)
        centred = values - jnp.mean(values, axis=-1, keepdims=True)
        spread = jnp.mean(centred * centred, axis=-1, keepdims=True)
        out_ref[...] = (
            centred * lax.rsqrt(spread + EPS) * (1.0 + scale_ref[...]) + shift_ref[...]
        ).astype(jnp.bfloat16)


def modulate(hidden, shift_mod, scale_mod):
    rows, width = hidden.shape
    return pl.pallas_call(
        modulate_kernel,
        in_specs=[whole()] * 3,
        out_specs=[whole()] * 2,
        out_shape=[jax.ShapeDtypeStruct((rows // 2, width), jnp.bfloat16)] * 2,
        compiler_params=params(),
        cost_estimate=cost(10 * rows * width, 4 * rows * width),
        name="modulate",
    )(hidden, shift_mod[None], scale_mod[None])


def heads_kernel(parts, aliased, *refs):
    x_refs = refs[:parts]
    w_ref, gain_ref = refs[parts : parts + 2]
    out_ref, rows_ref = refs[parts + 2 + aliased :]
    pair = pl.program_id(0)
    frames, _, tokens, _ = out_ref.shape

    @pl.when(pair == 0)
    def _():
        at = 0
        for ref in x_refs:
            rows_ref[at : at + ref.shape[0], :] = ref[...]
            at += ref.shape[0]

    weight = jnp.concatenate([w_ref[0, j] for j in range(3)], axis=1)
    projected = jnp.dot(rows_ref[...], weight, preferred_element_type=jnp.float32)
    gains = gain_ref[pair]
    for j in range(3):
        v = projected[:, j * HD : (j + 1) * HD]
        if j < 2:
            square_mean = jnp.mean(v * v, axis=-1, keepdims=True)
            v = v * lax.rsqrt(square_mean + EPS) * gains[j : j + 1]
        out_ref[:, 0, :, j * HD : (j + 1) * HD] = v.astype(jnp.bfloat16).reshape(
            frames, tokens, HD
        )


def heads_both_kernel(parts, aliased, *refs):
    x_refs = refs[:parts]
    w_ref, gain_ref = refs[parts : parts + 2]
    spatial_ref, temporal_ref, rows_ref = refs[parts + 2 + aliased :]
    pair = pl.program_id(0)
    frames, _, tokens, _ = spatial_ref.shape

    @pl.when(pair == 0)
    def _():
        at = 0
        for ref in x_refs:
            rows_ref[at : at + ref.shape[0], :] = ref[...]
            at += ref.shape[0]

    weight = jnp.concatenate([w_ref[0, j] for j in range(6)], axis=1)
    projected = jnp.dot(rows_ref[...], weight, preferred_element_type=jnp.float32)
    for kind, out_ref in enumerate((spatial_ref, temporal_ref)):
        gains = gain_ref[kind, pair]
        for j in range(3):
            at = (kind * 3 + j) * HD
            v = projected[:, at : at + HD]
            if j < 2:
                square_mean = jnp.mean(v * v, axis=-1, keepdims=True)
                v = v * lax.rsqrt(square_mean + EPS) * gains[j : j + 1]
            out_ref[:, 0, :, j * HD : (j + 1) * HD] = v.astype(jnp.bfloat16).reshape(
                frames, tokens, HD
            )


def heads_both(pieces, weight, norm_gain, first, buffers=None):
    parts = len(pieces)
    width = pieces[0].shape[1]
    rows = sum(piece.shape[0] for piece in pieces)
    pairs = weight.shape[0]
    frames = rows // BLK
    triple = 3 * HD
    in_specs = [pl.BlockSpec(piece.shape, lambda n: (0, 0)) for piece in pieces]
    in_specs += [
        pl.BlockSpec((1, 6, width, HD), lambda n: (n, 0, 0, 0)),
        pl.BlockSpec((2, pairs, 2, HD), lambda n: (0, 0, 0, 0)),
    ]
    args = list(pieces) + [weight, norm_gain]
    aliases = {}
    if buffers is not None:
        in_specs += [pl.BlockSpec(memory_space=pl.ANY)] * 2
        aliases = {len(args): 0, len(args) + 1: 1}
        args += list(buffers)
    out_spec = pl.BlockSpec((frames, 1, BLK, triple), lambda n: (first // frames, n, 0, 0))
    return pl.pallas_call(
        lambda *refs: heads_both_kernel(parts, 2 * (buffers is not None), *refs),
        grid=(pairs,),
        in_specs=in_specs,
        out_specs=[out_spec, out_spec],
        out_shape=[
            jax.ShapeDtypeStruct((4, slots, BLK, triple), jnp.bfloat16) for slots in (4, pairs)
        ],
        scratch_shapes=[pltpu.VMEM((rows, width), jnp.bfloat16)],
        input_output_aliases=aliases,
        compiler_params=params(WIDE),
        cost_estimate=cost(4 * rows * width * pairs * triple, width * pairs * triple * 4),
        name="qkv_both",
    )(*args)


def heads(pieces, weight, norm_gain, kind, slots, first, buffer=None):
    parts = len(pieces)
    width = pieces[0].shape[1]
    rows = sum(piece.shape[0] for piece in pieces)
    pairs = weight.shape[0]
    block = kind if weight.shape[1] > 3 else 0
    frames = rows // BLK
    triple = 3 * HD
    aliased = buffer is not None
    in_specs = [pl.BlockSpec(piece.shape, lambda n: (0, 0)) for piece in pieces]
    in_specs += [
        pl.BlockSpec((1, 3, width, HD), lambda n: (n, block, 0, 0)),
        pl.BlockSpec((pairs, 2, HD), lambda n: (0, 0, 0)),
    ]
    args = list(pieces) + [weight, norm_gain[kind]]
    aliases = {}
    if aliased:
        in_specs.append(pl.BlockSpec(memory_space=pl.ANY))
        aliases = {len(args): 0}
        args.append(buffer)

    def body(*refs):
        heads_kernel(parts, int(aliased), *refs)

    return pl.pallas_call(
        body,
        grid=(pairs,),
        in_specs=in_specs,
        out_specs=pl.BlockSpec((frames, 1, BLK, triple), lambda n: (first // frames, n, 0, 0)),
        out_shape=jax.ShapeDtypeStruct((4, slots, BLK, triple), jnp.bfloat16),
        scratch_shapes=[pltpu.VMEM((rows, width), jnp.bfloat16)],
        input_output_aliases=aliases,
        compiler_params=params(),
        cost_estimate=cost(2 * rows * width * pairs * triple, width * pairs * triple * 2),
        name="qkv_spatial" if kind == 0 else "qkv_temporal",
    )(*args)


def spatial_kernel(own_ref, other_ref, bias_ref, out_ref):
    blocks = own_ref.shape[0]
    rows = blocks * BLK
    shape = (blocks, BLK, HD)
    one_hot = lax.broadcasted_iota(jnp.int32, shape, 2) == lax.broadcasted_iota(jnp.int32, shape, 0)
    one_hot = jnp.where(one_hot, 1.0, 0.0).astype(jnp.bfloat16)
    queries = jnp.concatenate([own_ref[:, :, 0:HD], one_hot], axis=2).reshape(rows, 2 * HD)
    per_chunk = 4
    chunk = per_chunk * BLK
    ones = jnp.ones((chunk, HD), jnp.bfloat16)
    summed = jnp.zeros((rows, 2 * HD), jnp.float32)
    for side, ref in enumerate((own_ref, other_ref)):
        for at in range(0, blocks, per_chunk):
            row = side * blocks + at
            bias = jnp.concatenate(
                [
                    jnp.broadcast_to(bias_ref[row + i : row + i + 1, :], (BLK, HD))
                    for i in range(per_chunk)
                ],
                axis=0,
            ).astype(jnp.bfloat16)
            keys = ref[at : at + per_chunk, :, HD : 2 * HD].reshape(chunk, HD)
            values = ref[at : at + per_chunk, :, 2 * HD :].reshape(chunk, HD)
            scores = lax.dot_general(
                queries, jnp.concatenate([keys, bias], axis=1), (((1,), (1,)), ((), ())),
                preferred_element_type=jnp.float32,
            )
            summed = summed + jnp.dot(
                jnp.exp2(scores).astype(jnp.bfloat16), jnp.concatenate([values, ones], axis=1),
                preferred_element_type=jnp.float32,
            )
    out_ref[...] = (summed[:, :HD] / summed[:, HD:]).astype(jnp.bfloat16).reshape(shape)


def spatial_attention(own, other, bias):
    blocks, tokens, triple = own.shape
    total = 2 * blocks * tokens
    return pl.pallas_call(
        spatial_kernel,
        in_specs=[whole()] * 3,
        out_specs=whole(),
        out_shape=jax.ShapeDtypeStruct((blocks, tokens, HD), jnp.bfloat16),
        compiler_params=params(),
        cost_estimate=cost(
            8 * blocks * tokens * total * HD, 4 * blocks * tokens * triple, blocks * tokens * total
        ),
        name="spatial_attention",
    )(own, other, bias)


def temporal_kernel(qkv_ref, bias_ref, out_ref):
    frames, _, tokens, _ = qkv_ref.shape
    rows = frames * tokens
    queries = qkv_ref[:, 0, :, 0:HD].reshape(rows, HD)
    keys = qkv_ref[:, 0, :, HD : 2 * HD].reshape(rows, HD)
    values = qkv_ref[:, 0, :, 2 * HD :].reshape(rows, HD)
    values = jnp.concatenate([values, jnp.ones((rows, HD), jnp.bfloat16)], axis=1)
    scores = lax.dot_general(
        queries, keys, (((1,), (1,)), ((), ())), preferred_element_type=jnp.float32
    )
    scores = scores.reshape(frames, tokens, rows) + bias_ref[0]
    weights = jnp.exp2(scores).astype(jnp.bfloat16).reshape(rows, rows)
    summed = jnp.dot(weights, values, preferred_element_type=jnp.float32)
    result = (summed[:, :HD] / summed[:, HD:]).astype(jnp.bfloat16)
    out_ref[:, 0] = result.reshape(frames, tokens, HD)


def temporal_attention(qkv, bias):
    frames, pairs, tokens, triple = qkv.shape
    rows = frames * tokens
    return pl.pallas_call(
        temporal_kernel,
        grid=(pairs,),
        in_specs=[
            pl.BlockSpec((frames, 1, tokens, triple), lambda h: (0, h, 0, 0)),
            pl.BlockSpec((1, frames, 1, rows), lambda h: (h, 0, 0, 0)),
        ],
        out_specs=pl.BlockSpec((frames, 1, tokens, HD), lambda h: (0, h, 0, 0)),
        out_shape=jax.ShapeDtypeStruct((frames, pairs, tokens, HD), jnp.bfloat16),
        compiler_params=params(),
        cost_estimate=cost(6 * pairs * rows * rows * HD, 2 * frames * pairs * tokens * triple),
        name="temporal_attention",
    )(qkv, bias)


OWN_SLOT = {0: 0, 1: 2, -1: 3}
FAR_SLOT = {0: 0, 1: 2, -1: 1}


def project_kernel(targets, groups, *refs):
    heads_count = 2 * len(groups)
    head_refs, w_ref = refs[:heads_count], refs[heads_count]
    rest, rows_ref = refs[heads_count + 1 : -1], refs[-1]
    step, steps = pl.program_id(0), pl.num_programs(0)
    shards, _, pairs, kinds, columns, _ = w_ref.shape
    depth = pairs * kinds * HD

    @pl.when(step == 0)
    def _():
        for number, target in enumerate(targets):
            for at_group, group in enumerate(groups):
                slot = (OWN_SLOT, FAR_SLOT)[group][target]
                for kind in range(kinds):
                    ref = head_refs[2 * at_group + kind]
                    for pair in range(pairs):
                        at = at_group * depth + (pair * kinds + kind) * HD
                        rows_ref[number, :, at : at + HD] = ref[slot, pair]

    weight = jnp.concatenate(
        [
            w_ref[:, at_group, pair, kind].reshape(shards * columns, HD)
            for at_group in range(len(groups))
            for pair in range(pairs)
            for kind in range(kinds)
        ],
        axis=1,
    )
    rows = rows_ref[step * len(targets) // steps]
    product = lax.dot_general(
        rows, weight, (((1,), (1,)), ((), ())), preferred_element_type=jnp.float32
    )
    if len(rest) == 1:
        rest[0][...] = product.astype(rest[0].dtype)
        return
    partial_ref, low_ref, high_ref = rest
    product = (product + partial_ref[...]).astype(jnp.bfloat16)

    @pl.when(step < steps // 2)
    def _():
        low_ref[...] = product

    @pl.when(step >= steps // 2)
    def _():
        high_ref[...] = product


def project(name, targets, groups, head_arrays, weight, dtype, limit, partial=None):
    shards, _, pairs, kinds, shard, _ = weight.shape
    per_step = 8
    steps, width = shards // per_step, per_step * shard
    depth = len(groups) * kinds * pairs * HD
    first = groups[0] // len(groups)
    column = pl.BlockSpec((BLK, width), lambda n: (0, n))
    partials = [] if partial is None else [partial]
    if partial is None:
        out_specs = column
        out_shape = jax.ShapeDtypeStruct((BLK, steps * width), dtype)
    else:
        out_specs = [
            pl.BlockSpec((BLK, width), lambda n: (0, jnp.minimum(n, steps // 2 - 1))),
            pl.BlockSpec((BLK, width), lambda n: (0, jnp.maximum(n - steps // 2, 0))),
        ]
        out_shape = [jax.ShapeDtypeStruct((BLK, steps // 2 * width), dtype)] * 2
    return pl.pallas_call(
        lambda *refs: project_kernel(targets, groups, *refs),
        grid=(steps,),
        in_specs=[pl.BlockSpec(array.shape, lambda n: (0, 0, 0, 0)) for array in head_arrays]
        + [
            pl.BlockSpec(
                (per_step, len(groups), pairs, kinds, shard, HD),
                lambda n: (n, first, 0, 0, 0, 0),
            )
        ]
        + [column] * len(partials),
        out_specs=out_specs,
        out_shape=out_shape,
        scratch_shapes=[pltpu.VMEM((len(targets), BLK, depth), jnp.bfloat16)],
        compiler_params=params(limit),
        cost_estimate=cost(2 * BLK * steps * width * depth, 2 * steps * width * depth),
        name=name,
    )(*head_arrays, weight, *partials)


def combine_kernel(own_ref, low_ref, high_ref, gate_ref, out_ref):
    step, steps = pl.program_id(0), pl.num_programs(0)

    def write(ref):
        branch = own_ref[...].astype(jnp.float32) + ref[...].astype(jnp.float32)
        out_ref[...] = (gate_ref[...] * branch).astype(jnp.bfloat16)

    @pl.when(step < steps // 2)
    def _():
        write(low_ref)

    @pl.when(step >= steps // 2)
    def _():
        write(high_ref)


def combine(own, low, high, gate):
    rows, width = own.shape
    steps = 2
    each = width // steps
    column = pl.BlockSpec((rows, each), lambda n: (0, n))
    return pl.pallas_call(
        combine_kernel,
        grid=(steps,),
        in_specs=[
            column,
            pl.BlockSpec((rows, each), lambda n: (0, jnp.minimum(n, steps // 2 - 1))),
            pl.BlockSpec((rows, each), lambda n: (0, jnp.maximum(n - steps // 2, 0))),
            pl.BlockSpec((1, each), lambda n: (0, n)),
        ],
        out_specs=column,
        out_shape=jax.ShapeDtypeStruct((rows, width), jnp.bfloat16),
        compiler_params=params(),
        cost_estimate=cost(3 * rows * width, 10 * rows * width),
        name="combine",
    )(own, low, high, gate[None])


def local(
    hidden_in,
    shift_mod,
    scale_mod,
    gate_mod,
    w_qkv,
    norm_gain,
    w_out,
    spatial_mask,
    temporal_mask,
    frame_order,
):
    tokens = hidden_in.shape[1]
    pairs = w_qkv.shape[1]
    y, x, core, z = (lax.axis_index(name) for name in ("y", "x", "core", "frm"))
    chips = lax.axis_size("y") * lax.axis_size("x")
    planes = lax.axis_size("frm")
    chip = y * lax.axis_size("x") + x
    seq_index = chip * 2 + core

    def along_z(value, shift):
        return lax.ppermute(value, "frm", [(i, (i + shift) % planes) for i in range(planes)])

    def swap_cores(value):
        return lax.ppermute(value, "core", [(0, 1), (1, 0)])

    with jax.named_scope("modulate"):
        own = modulate(hidden_in[0], shift_mod, scale_mod)

    with jax.named_scope("gather_w_out"):
        turned = jnp.transpose(w_out, (0, 1, 3, 2))
        (low, high), turned_far = lax.optimization_barrier((own, along_z(turned, 2)))
        out_weight = jnp.stack([turned, turned_far])
        out_weight = lax.all_gather(out_weight, ("y", "x", "core"), axis=0, tiled=False)

    with jax.named_scope("qkv"):
        weight = jnp.transpose(w_qkv, (1, 2, 0, 3))
        factor = jnp.array([LOG2E / math.sqrt(HD), 1.0], jnp.float32)
        norm_gain = jnp.transpose(norm_gain.reshape(pairs, 2, 2, HD), (1, 0, 2, 3))
        norm_gain = norm_gain * factor[None, None, :, None]
        before_low, after_high = along_z(low, 1), along_z(high, -1)
        before_high, after_low = along_z(high, 1), along_z(low, -1)
        spatial, temporal = heads_both([low, high], weight, norm_gain, 0)
        before_low, after_high, spatial, temporal = lax.optimization_barrier(
            (before_low, after_high, spatial, temporal)
        )
        far = [along_z(before_low, 1), along_z(after_high, -1)]
        spatial, temporal = heads_both(
            [after_low, after_high, before_low, before_high],
            weight,
            norm_gain,
            2,
            (spatial, temporal),
        )
        far, spatial, temporal = lax.optimization_barrier((far, spatial, temporal))
        spatial = heads(far, weight, norm_gain, 0, 4, 1, spatial)
        spatial, far = lax.optimization_barrier((spatial, far))
        temporal = heads(far, weight, norm_gain, 1, pairs, 1, temporal)

    frames = (z + jnp.array(REL, jnp.int32)) % planes

    with jax.named_scope("temporal"):
        order = frame_order.astype(jnp.float32)[frames]
        distance = jnp.abs(order[:, None] - order[None, :])
        pair_global = (z * pairs + jnp.arange(pairs, dtype=jnp.int32)).astype(jnp.float32)
        slope = jnp.exp2(-(pair_global + 1.0) * 2.0 / HP)
        tmask = lax.dynamic_index_in_dim(temporal_mask, seq_index, 1, keepdims=False)
        tmask = tmask[:, frames][:, :, frames]
        bias_t = jnp.where(tmask > 0, -slope[:, None, None] * distance[None] * LOG2E, OFF)
        bias_t = jnp.repeat(bias_t, tokens, axis=2)[:, :, None, :]
        temporal_out = temporal_attention(temporal, bias_t)
        temporal_far = along_z(temporal_out[1:], 2)

    with jax.named_scope("spatial"):
        smask = lax.dynamic_index_in_dim(
            spatial_mask, jnp.minimum(x, pairs - 1), 0, keepdims=False
        )
        slot_frame = (z + jnp.array(REL, jnp.int32)[y]) % planes
        smask = lax.dynamic_index_in_dim(smask, slot_frame, 0, keepdims=False)
        smask = smask.reshape(chips, 2, chips, 2)
        smask = lax.dynamic_index_in_dim(smask, core, 1, keepdims=False)
        own_keys = lax.dynamic_index_in_dim(smask, core, 2, keepdims=False)
        other_keys = lax.dynamic_index_in_dim(smask, 1 - core, 2, keepdims=False)
        smask = jnp.concatenate([own_keys, other_keys], axis=1).T
        bias_s = jnp.where(smask > 0, 0.0, OFF).astype(jnp.float32)
        bias_s = jnp.pad(bias_s, ((0, 0), (0, HD - chips)))
        mine = lax.all_to_all(
            spatial.reshape(chips, tokens, 3 * HD), ("y", "x"), 0, 0, tiled=True
        )
        mine, temporal_out, temporal_far, bias_s, out_weight = lax.optimization_barrier(
            (mine, temporal_out, temporal_far, bias_s, out_weight)
        )
        other = swap_cores(mine)
        spatial_out = spatial_attention(mine, other, bias_s)
        spatial_out = lax.all_to_all(spatial_out, ("y", "x"), 0, 0, tiled=True)
        spatial_out = spatial_out.reshape(4, 4, tokens, HD)
        spatial_far = along_z(spatial_out[1:, :pairs], 2)

    with jax.named_scope("project"):
        own_heads, far_heads = [spatial_out, temporal_out], [spatial_far, temporal_far]
        sent = project(
            "project_sent_own_group", (1, -1), (0,), own_heads, out_weight, jnp.float32, WIDE
        )
        low, high = project(
            "project_sent", (1, -1), (1,), far_heads, out_weight, jnp.bfloat16, NARROW, sent
        )
        low = along_z(low, 1)
        high = along_z(high, -1)
        kept = project(
            "project_kept", (0,), (0, 1), own_heads + far_heads, out_weight, jnp.bfloat16, NARROW
        )
        return combine(kept, low, high, gate_mod)[None]


def solution(mesh):
    split = Mesh(mesh.devices.reshape(4, 4, 2, 4), ("y", "x", "core", "frm"))
    seq = ("y", "x", "core")
    placed = (
        P("frm", seq, None),
        P(),
        P(),
        P(),
        P(None, "frm", None, None),
        P("frm", None, None),
        P("frm", None, None, seq),
        P("frm", None, None, None),
        P("frm", None, None, None),
        P(),
    )
    return jax.shard_map(
        local, mesh=split, in_specs=placed, out_specs=P("frm", seq, None), check_vma=False
    )
```

profile of v0, /device:TPU:0, one launch (start us, length us, event | category | flops | bytes accessed | tf_op | source)
XLA Modules:
  0.0 177.8 jit_solution(11721967952974880267)
XLA Ops:
  6.5 4.0 %collective-permute-start = (bf16[3,2,160,128]{3,2,1,0:T(8,128)(2,1)}, bf16[3,2,160,128]{3,2,1,0:T(8,128)(2,1)S(1)}, u32[]{:S(2)}, u32[]{:S(2)}) collective-permute-start(bf16[3,2,160,128]{3,2,1,0:T(8,128)(2,1)} %bitcast.49), channel_id=1, source_target_pairs={{0,2},{1,3},{2,0},{3,1},{4,6},{5,7},{6,4},{7,5},{8,10},{9,11},{10,... | collective-permute-start | bytes 737288 | tf_op jit(solution)/shard_map/gather_w_out/ppermute | solution.py:418
  10.6 1.3 copy-done.1
  11.9 0.7 copy-done.3
  12.6 0.7 copy-done.4
  13.4 1.8 %modulate.1 = (bf16[64,5120]{1,0:T(8,128)(2,1)}, bf16[64,5120]{1,0:T(8,128)(2,1)S(1)}) custom-call(bf16[128,5120]{1,0:T(8,128)(2,1)S(1)} %bitcast.40, f32[1,5120]{1,0:T(1,128)S(1)} %bitcast.43, f32[1,5120]{1,0:T(1,128)S(1)} %bitcast.44), custom_call_target="tpu_custom_call" | custom-call | flops 6553600 | bytes 2621440 | tf_op jit(solution)/shard_map/modulate/modulate/pallas_call | solution.py:46
  15.2 1.6 collective-permute-done
  16.8 1.8 pad_maximum_fusion
  18.5 1.4 collective-permute-start.1
  19.9 2.2 %collective-permute-start.2 = (bf16[64,5120]{1,0:T(8,128)(2,1)S(1)}, bf16[64,5120]{1,0:T(8,128)(2,1)}, u32[]{:S(2)}, u32[]{:S(2)}) collective-permute-start(bf16[64,5120]{1,0:T(8,128)(2,1)S(1)} %get-tuple-element.35.refs_1_), channel_id=1, source_target_pairs={{0,3},{1,0},{2,1},{3,2},{4,7},{5,4},{6,5},{7,6},{8,11},{9,8},{10,9... | collective-permute-start | bytes 1966088 | tf_op jit(solution)/shard_map/qkv/ppermute | solution.py:418
  22.1 1.9 %collective-permute-start.5 = (bf16[64,5120]{1,0:T(8,128)(2,1)}, bf16[64,5120]{1,0:T(8,128)(2,1)}, u32[]{:S(2)}, u32[]{:S(2)}) collective-permute-start(bf16[64,5120]{1,0:T(8,128)(2,1)} %get-tuple-element.34.refs_0_), channel_id=1, source_target_pairs={{0,3},{1,0},{2,1},{3,2},{4,7},{5,4},{6,5},{7,6},{8,11},{9,8},{10,9... | collective-permute-start | bytes 1966088 | tf_op jit(solution)/shard_map/qkv/ppermute | solution.py:418
  24.0 0.1 collective-permute-start.6
  24.2 10.5 %qkv_both.2 = (bf16[4,4,128,384]{3,2,1,0:T(8,128)(2,1)}, bf16[4,3,128,384]{3,2,1,0:T(8,128)(2,1)S(1)}) custom-call(bf16[64,5120]{1,0:T(8,128)(2,1)} %get-tuple-element.34.refs_0_, bf16[64,5120]{1,0:T(8,128)(2,1)S(1)} %get-tuple-element.35.refs_1_, bf16[3,6,5120,128]{3,2,1,0:T(8,128)(2,1)} %bitcast.45, f32[2,3,2,128]{3,2,1,0:T(2,128)S(1)} %fusion.refs_3_.refs_5_), custom_call_target="tpu_custom_call" | custom-call | flops 3019898880 | bytes 23592960 | tf_op jit(solution)/shard_map/qkv/qkv_both/pallas_call | solution.py:132
  34.7 3.2 %collective-permute-done.1.refs_2_ = bf16[64,5120]{1,0:T(8,128)(2,1)} collective-permute-done((bf16[64,5120]{1,0:T(8,128)(2,1)}, bf16[64,5120]{1,0:T(8,128)(2,1)}, u32[]{:S(2)}, u32[]{:S(2)}) %collective-permute-start.1) | collective-permute-done | bytes 655392 | tf_op jit(solution)/shard_map/qkv/ppermute | solution.py:418
  38.0 1.6 collective-permute-start.3
  39.6 1.6 collective-permute-start.4
  41.2 10.5 %collective-permute-done.5.refs_0_ = bf16[64,5120]{1,0:T(8,128)(2,1)} collective-permute-done((bf16[64,5120]{1,0:T(8,128)(2,1)}, bf16[64,5120]{1,0:T(8,128)(2,1)}, u32[]{:S(2)}, u32[]{:S(2)}) %collective-permute-start.5) | collective-permute-done | bytes 655392 | tf_op jit(solution)/shard_map/qkv/ppermute | solution.py:418
  51.7 0.3 collective-permute-done.6.refs_3_
  52.0 14.3 %qkv_both.3 = (bf16[4,4,128,384]{3,2,1,0:T(8,128)(2,1)}, bf16[4,3,128,384]{3,2,1,0:T(8,128)(2,1)S(1)}) custom-call(bf16[64,5120]{1,0:T(8,128)(2,1)} %collective-permute-done.5.refs_0_, bf16[64,5120]{1,0:T(8,128)(2,1)} %collective-permute-done.2.refs_1_, ...), custom_call_target="tpu_custom_call", output_to_operand_aliasing={{0}: (6, {}), {1}: (7, {})} | custom-call | flops 6039797760 | bytes 23592960 | tf_op jit(solution)/shard_map/qkv/qkv_both/pallas_call | solution.py:132
  66.3 7.2 %qkv_spatial.1 = bf16[4,4,128,384]{3,2,1,0:T(8,128)(2,1)} custom-call(bf16[64,5120]{1,0:T(8,128)(2,1)S(1)} %collective-permute-done.3.refs_0_, bf16[64,5120]{1,0:T(8,128)(2,1)S(1)} %collective-permute-done.4.refs_1_, bf16[3,6,5120,128]{3,2,1,0:T(8,128)(2,1)} %bitcast.47, f32[3,2,128]{2,1,0:T(2,128)S(1)} %get-tuple-element.62.refs_3_, ...), custom_call_target="tpu_custom_call", output_to_operand_aliasing={{}: (4, {})} | custom-call | flops 1509949440 | bytes 11796480 | tf_op jit(solution)/shard_map/qkv/qkv_spatial/pallas_call | solution.py:172
  73.5 7.2 %all-to-all-start = ((bf16[16,128,384]{2,1,0:T(8,128)(2,1)}), bf16[16,128,384]{2,1,0:T(8,128)(2,1)}, u32[]{:S(2)}, u32[]{:S(2)}) async-start(bf16[16,128,384]{2,1,0:T(8,128)(2,1)} %bitcast.8), calls=%async_computation | async-start | bytes 3145728 | tf_op jit(solution)/shard_map/spatial/all_to_all | solution.py:483
  80.8 0.6 dynamic_slice.23
  82.1 0.2 copy.30
  82.3 0.6 gather_fusion
  82.9 0.1 copy.26
  83.0 0.6 gather_fusion.1
  83.6 0.6 gather_fusion.2
  84.4 0.1 copy.27
  84.5 6.2 %qkv_temporal.1.qkv_ref = bf16[4,3,128,384]{3,2,1,0:T(8,128)(2,1)S(1)} custom-call(bf16[64,5120]{1,0:T(8,128)(2,1)S(1)} %collective-permute-done.3.refs_0_, bf16[64,5120]{1,0:T(8,128)(2,1)S(1)} %collective-permute-done.4.refs_1_, bf16[3,6,5120,128]{3,2,1,0:T(8,128)(2,1)} %bitcast.48, ...), custom_call_target="tpu_custom_call", output_to_operand_aliasing={{}: (4, {})} | custom-call | flops 1509949440 | bytes 11796480 | tf_op jit(solution)/shard_map/qkv/qkv_temporal/pallas_call | solution.py:172
  90.8 1.9 %temporal_attention.1.refs_1_ = bf16[4,3,128,128]{3,2,1,0:T(8,128)(2,1)S(1)} custom-call(bf16[4,3,128,384]{3,2,1,0:T(8,128)(2,1)S(1)} %qkv_temporal.1.qkv_ref, f32[3,4,1,512]{3,2,1,0:T(1,128)S(1)} %bitcast.41), custom_call_target="tpu_custom_call" | custom-call | flops 603979776 | bytes 1179648 | tf_op jit(solution)/shard_map/temporal/temporal_attention/pallas_call | solution.py:256
  92.7 3.5 %collective-permute-start.7 = (bf16[3,3,128,128]{3,2,1,0:T(8,128)(2,1)S(1)}, bf16[3,3,128,128]{3,2,1,0:T(8,128)(2,1)S(1)}, u32[]{:S(2)}, u32[]{:S(2)}) collective-permute-start(bf16[3,3,128,128]{3,2,1,0:T(8,128)(2,1)S(1)} %slice.24), channel_id=1, source_target_pairs={{0,2},{1,3},{2,0},{3,1},{4,6},{5,7},{6,4},{7,5},{8,10},{9,11},{10,... | collective-permute-start | bytes 884744 | tf_op jit(solution)/shard_map/temporal/ppermute | solution.py:418
  96.2 0.2 reshape.65
  96.3 0.1 constant_dynamic-slice_fusion.1
  96.5 0.2 copy.28
  96.7 0.2 copy.29
  96.9 4.1 %collective-permute-done.7.refs_3_.refs_1_ = bf16[3,3,128,128]{3,2,1,0:T(8,128)(2,1)S(1)} collective-permute-done((bf16[3,3,128,128]{3,2,1,0:T(8,128)(2,1)S(1)}, bf16[3,3,128,128]{3,2,1,0:T(8,128)(2,1)S(1)}, u32[]{:S(2)}, u32[]{:S(2)}) %collective-permute-start.7) | collective-permute-done | bytes 294944 | tf_op jit(solution)/shard_map/temporal/ppermute | solution.py:418
  101.0 7.4 %all-to-all-done.own_ref = bf16[16,128,384]{2,1,0:T(8,128)(2,1)} async-done(((bf16[16,128,384]{2,1,0:T(8,128)(2,1)}), bf16[16,128,384]{2,1,0:T(8,128)(2,1)}, u32[]{:S(2)}, u32[]{:S(2)}) %all-to-all-start) | async-done | bytes 1572896 | tf_op jit(solution)/shard_map/spatial/all_to_all | solution.py:483
  108.4 3.6 %collective-permute-done.8.other_ref = bf16[16,128,384]{2,1,0:T(8,128)(2,1)S(1)} collective-permute-done((bf16[16,128,384]{2,1,0:T(8,128)(2,1)}, bf16[16,128,384]{2,1,0:T(8,128)(2,1)S(1)}, u32[]{:S(2)}, u32[]{:S(2)}) %collective-permute-start.8) | collective-permute-done | bytes 1572896 | tf_op jit(solution)/shard_map/spatial/ppermute | solution.py:421
  112.0 11.7 %spatial_attention.1 = bf16[16,128,128]{2,1,0:T(8,128)(2,1)S(1)} custom-call(bf16[16,128,384]{2,1,0:T(8,128)(2,1)} %all-to-all-done.own_ref, bf16[16,128,384]{2,1,0:T(8,128)(2,1)S(1)} %collective-permute-done.8.other_ref, f32[32,128]{1,0:T(8,128)S(1)} %pad.4.bias_ref), custom_call_target="tpu_custom_call" | custom-call | flops 8589934592 | bytes 3145728 | tf_op jit(solution)/shard_map/spatial/spatial_attention/pallas_call | solution.py:223
  123.7 15.9 %all_to_all.10 = bf16[16,128,128]{2,1,0:T(8,128)(2,1)S(1)} all-to-all(bf16[16,128,128]{2,1,0:T(8,128)(2,1)S(1)} %spatial_attention.1), channel_id=1, replica_groups=mesh['y'=4,'x'=4,'core'=2,'frm'=4] {'y','x'}, dimensions={0} | all-to-all | bytes 1048576 | tf_op jit(solution)/shard_map/spatial/all_to_all | solution.py:491
  139.6 3.2 %collective-permute-start.9 = (bf16[3,3,128,128]{3,2,1,0:T(8,128)(2,1)S(1)}, bf16[3,3,128,128]{3,2,1,0:T(8,128)(2,1)S(1)}, u32[]{:S(2)}, u32[]{:S(2)}) collective-permute-start(bf16[3,3,128,128]{3,2,1,0:T(8,128)(2,1)S(1)} %slice.25), channel_id=1, source_target_pairs={{0,2},{1,3},{2,0},{3,1},{4,6},{5,7},{6,4},{7,5},{8,10},{9,11},{10,... | collective-permute-start | bytes 884744 | tf_op jit(solution)/shard_map/spatial/ppermute | solution.py:418
  142.9 5.8 %project_sent_own_group.1.refs_3_ = f32[128,5120]{1,0:T(8,128)S(1)} custom-call(bf16[4,4,128,128]{3,2,1,0:T(8,128)(2,1)S(1)} %bitcast.38, bf16[4,3,128,128]{3,2,1,0:T(8,128)(2,1)S(1)} %temporal_attention.1.refs_1_, bf16[32,2,3,2,160,128]{5,4,3,2,1,0:T(8,128)(2,1)} %bitcast.32), custom_call_target="tpu_custom_call" | custom-call | flops 1006632960 | bytes 7864320 | tf_op jit(solution)/shard_map/project/project_sent_own_group/pallas_call | solution.py:339
  148.7 0.3 collective-permute-done.9.refs_2_.refs_0_
  149.0 4.3 %project_sent.1 = (bf16[128,2560]{1,0:T(8,128)(2,1)S(1)}, bf16[128,2560]{1,0:T(8,128)(2,1)S(1)}) custom-call(bf16[3,3,128,128]{3,2,1,0:T(8,128)(2,1)S(1)} %collective-permute-done.9.refs_2_.refs_0_, bf16[3,3,128,128]{3,2,1,0:T(8,128)(2,1)S(1)} %collective-permute-done.7.refs_3_.refs_1_, bf16[32,2,3,2,160,128]{5,4,3,2,1,0:T(8,128)(2,1)S(1)} %bitcast.35, ...), custom_call_target="tpu_custom_call" | custom-call | flops 1006632960 | bytes 7864320 | tf_op jit(solution)/shard_map/project/project_sent/pallas_call | solution.py:339
  153.4 1.6 collective-permute-start.10
  155.0 1.7 collective-permute-start.11
  156.7 5.7 %project_kept.1.own_ref = bf16[128,5120]{1,0:T(8,128)(2,1)S(1)} custom-call(bf16[4,4,128,128]{3,2,1,0:T(8,128)(2,1)S(1)} %bitcast.39, bf16[4,3,128,128]{3,2,1,0:T(8,128)(2,1)S(1)} %temporal_attention.1.refs_1_, bf16[3,3,128,128]{3,2,1,0:T(8,128)(2,1)S(1)} %collective-permute-done.9.refs_2_.refs_0_, ...), custom_call_target="tpu_custom_call" | custom-call | flops 2013265920 | bytes 15728640 | tf_op jit(solution)/shard_map/project/project_kept/pallas_call | solution.py:339
  162.4 7.2 %collective-permute-done.10.low_ref = bf16[128,2560]{1,0:T(8,128)(2,1)S(1)} collective-permute-done((bf16[128,2560]{1,0:T(8,128)(2,1)S(1)}, bf16[128,2560]{1,0:T(8,128)(2,1)S(1)}, u32[]{:S(2)}, u32[]{:S(2)}) %collective-permute-start.10) | collective-permute-done | bytes 655392 | tf_op jit(solution)/shard_map/project/ppermute | solution.py:418
  169.6 1.4 combine.1
  (49 shorter events, 0.5 us)
Async XLA Ops:
  6.5 89.6 %copy-start = (s32[3,4,32,32]{3,2,1,0:T(8,128)S(1)}, s32[3,4,32,32]{3,2,1,0:T(8,128)}, u32[]{:S(2)}) copy-start(s32[3,4,32,32]{3,2,1,0:T(8,128)} %param.20) | copy-start | bytes 147460
  6.5 17.6 %copy-start.7 = (f32[2]{0:T(128)S(1)}, f32[2]{0:T(128)}, u32[]{:S(2)}) copy-start(f32[2]{0:T(128)} %constant.151.clone) | copy-start | bytes 28
  6.5 17.6 %copy-start.6 = (f32[3,4,128]{2,1,0:T(4,128)S(1)}, f32[3,4,128]{2,1,0:T(4,128)}, u32[]{:S(2)}) copy-start(f32[3,4,128]{2,1,0:T(4,128)} %param.18) | copy-start | bytes 18436
  6.5 101.8 %all-gather.3.cloned.1.call-start = ((), (), s32[]{:S(2)}) async-start(), calls=%async_computation.2 | async-start | bytes 16220160 | tf_op jit(solution)/shard_map/gather_w_out/all_gather | solution.py:430
  6.5 10.2 %collective-permute-start = (bf16[3,2,160,128]{3,2,1,0:T(8,128)(2,1)}, bf16[3,2,160,128]{3,2,1,0:T(8,128)(2,1)S(1)}, u32[]{:S(2)}, u32[]{:S(2)}) collective-permute-start(bf16[3,2,160,128]{3,2,1,0:T(8,128)(2,1)} %bitcast.49), channel_id=1, source_target_pairs={{0,2},{1,3},{2,0},{3,1},{4,6},{5,7},{6,4},{7,5},{8,10},{9,11},{10,... | collective-permute-start | bytes 737288 | tf_op jit(solution)/shard_map/gather_w_out/ppermute | solution.py:418
  10.6 1.3 copy-start.1
  11.9 0.7 copy-start.3
  12.6 0.7 copy-start.4
  18.5 19.4 %collective-permute-start.1 = (bf16[64,5120]{1,0:T(8,128)(2,1)}, bf16[64,5120]{1,0:T(8,128)(2,1)}, u32[]{:S(2)}, u32[]{:S(2)}) collective-permute-start(bf16[64,5120]{1,0:T(8,128)(2,1)} %get-tuple-element.34.refs_0_), channel_id=1, source_target_pairs={{0,1},{1,2},{2,3},{3,0},{4,5},{5,6},{6,7},{7,4},{8,9},{9,10},{10,1... | collective-permute-start | bytes 1966088 | tf_op jit(solution)/shard_map/qkv/ppermute | solution.py:418
  19.9 18.1 %collective-permute-start.2 = (bf16[64,5120]{1,0:T(8,128)(2,1)S(1)}, bf16[64,5120]{1,0:T(8,128)(2,1)}, u32[]{:S(2)}, u32[]{:S(2)}) collective-permute-start(bf16[64,5120]{1,0:T(8,128)(2,1)S(1)} %get-tuple-element.35.refs_1_), channel_id=1, source_target_pairs={{0,3},{1,0},{2,1},{3,2},{4,7},{5,4},{6,5},{7,6},{8,11},{9,8},{10,9... | collective-permute-start | bytes 1966088 | tf_op jit(solution)/shard_map/qkv/ppermute | solution.py:418
  22.1 29.6 %collective-permute-start.5 = (bf16[64,5120]{1,0:T(8,128)(2,1)}, bf16[64,5120]{1,0:T(8,128)(2,1)}, u32[]{:S(2)}, u32[]{:S(2)}) collective-permute-start(bf16[64,5120]{1,0:T(8,128)(2,1)} %get-tuple-element.34.refs_0_), channel_id=1, source_target_pairs={{0,3},{1,0},{2,1},{3,2},{4,7},{5,4},{6,5},{7,6},{8,11},{9,8},{10,9... | collective-permute-start | bytes 1966088 | tf_op jit(solution)/shard_map/qkv/ppermute | solution.py:418
  24.0 28.0 %collective-permute-start.6 = (bf16[64,5120]{1,0:T(8,128)(2,1)S(1)}, bf16[64,5120]{1,0:T(8,128)(2,1)}, u32[]{:S(2)}, u32[]{:S(2)}) collective-permute-start(bf16[64,5120]{1,0:T(8,128)(2,1)S(1)} %get-tuple-element.35.refs_1_), channel_id=1, source_target_pairs={{0,1},{1,2},{2,3},{3,0},{4,5},{5,6},{6,7},{7,4},{8,9},{9,10},{10,1... | collective-permute-start | bytes 1966088 | tf_op jit(solution)/shard_map/qkv/ppermute | solution.py:418
  38.0 28.4 %collective-permute-start.3 = (bf16[64,5120]{1,0:T(8,128)(2,1)}, bf16[64,5120]{1,0:T(8,128)(2,1)S(1)}, u32[]{:S(2)}, u32[]{:S(2)}) collective-permute-start(bf16[64,5120]{1,0:T(8,128)(2,1)} %collective-permute-done.1.refs_2_), channel_id=1, source_target_pairs={{0,1},{1,2},{2,3},{3,0},{4,5},{5,6},{6,7},{7,4},{8,9},{9,10},{10,1... | collective-permute-start | bytes 1966088 | tf_op jit(solution)/shard_map/qkv/ppermute | solution.py:418
  39.6 26.8 %collective-permute-start.4 = (bf16[64,5120]{1,0:T(8,128)(2,1)}, bf16[64,5120]{1,0:T(8,128)(2,1)S(1)}, u32[]{:S(2)}, u32[]{:S(2)}) collective-permute-start(bf16[64,5120]{1,0:T(8,128)(2,1)} %collective-permute-done.2.refs_1_), channel_id=1, source_target_pairs={{0,3},{1,0},{2,1},{3,2},{4,7},{5,4},{6,5},{7,6},{8,11},{9,8},{10,9... | collective-permute-start | bytes 1966088 | tf_op jit(solution)/shard_map/qkv/ppermute | solution.py:418
  73.5 7.2 %copy-start.5 = (s32[3,32,4,4]{1,3,2,0:T(4,128)S(1)}, s32[3,32,4,4]{1,3,2,0:T(4,128)}, u32[]{:S(2)}) copy-start(s32[3,32,4,4]{1,3,2,0:T(4,128)} %param.21) | copy-start | bytes 18436
  73.5 7.3 %copy-start.9 = (s32[4]{0:T(128)S(1)}, s32[4]{0:T(128)}, u32[]{:S(2)}) copy-start(s32[4]{0:T(128)} %constant.152.clone) | copy-start | bytes 52
  73.5 10.0 %copy-start.8 = (s32[4]{0:T(128)S(1)}, s32[4]{0:T(128)}, u32[]{:S(2)}) copy-start(s32[4]{0:T(128)} %param.22) | copy-start | bytes 52
  73.5 34.9 %all-to-all-start = ((bf16[16,128,384]{2,1,0:T(8,128)(2,1)}), bf16[16,128,384]{2,1,0:T(8,128)(2,1)}, u32[]{:S(2)}, u32[]{:S(2)}) async-start(bf16[16,128,384]{2,1,0:T(8,128)(2,1)} %bitcast.8), calls=%async_computation | async-start | bytes 3145728 | tf_op jit(solution)/shard_map/spatial/all_to_all | solution.py:483
  92.7 8.3 %collective-permute-start.7 = (bf16[3,3,128,128]{3,2,1,0:T(8,128)(2,1)S(1)}, bf16[3,3,128,128]{3,2,1,0:T(8,128)(2,1)S(1)}, u32[]{:S(2)}, u32[]{:S(2)}) collective-permute-start(bf16[3,3,128,128]{3,2,1,0:T(8,128)(2,1)S(1)} %slice.24), channel_id=1, source_target_pairs={{0,2},{1,3},{2,0},{3,1},{4,6},{5,7},{6,4},{7,5},{8,10},{9,11},{10,... | collective-permute-start | bytes 884744 | tf_op jit(solution)/shard_map/temporal/ppermute | solution.py:418
  108.4 3.6 %collective-permute-start.8 = (bf16[16,128,384]{2,1,0:T(8,128)(2,1)}, bf16[16,128,384]{2,1,0:T(8,128)(2,1)S(1)}, u32[]{:S(2)}, u32[]{:S(2)}) collective-permute-start(bf16[16,128,384]{2,1,0:T(8,128)(2,1)} %all-to-all-done.own_ref), channel_id=1, source_target_pairs={{0,4},{4,0},{1,5},{5,1},{2,6},{6,2},{3,7},{7,3},{8,12},{12,8},{9,1... | collective-permute-start | bytes 4718600 | tf_op jit(solution)/shard_map/spatial/ppermute | solution.py:421
  112.0 37.0 %slice-start = ((s8[15728640]{0:T(1024)(128)(4,1)}), s8[4194304]{0:T(1024)(128)(4,1)S(1)}, s32[]{:S(2)}) async-start(s8[15728640]{0:T(1024)(128)(4,1)} %bitcast.33), calls=%async_computation.3 | async-start | bytes 8388608
  112.0 37.0 %slice-start.1 = ((s8[15728640]{0:T(1024)(128)(4,1)}), s8[4194304]{0:T(1024)(128)(4,1)S(1)}, s32[]{:S(2)}) async-start(s8[15728640]{0:T(1024)(128)(4,1)} %bitcast.33), calls=%async_computation.4 | async-start | bytes 8388608
  112.0 37.0 %slice-start.2 = ((s8[15728640]{0:T(1024)(128)(4,1)}), s8[4194304]{0:T(1024)(128)(4,1)S(1)}, s32[]{:S(2)}) async-start(s8[15728640]{0:T(1024)(128)(4,1)} %bitcast.33), calls=%async_computation.5 | async-start | bytes 8388608
  139.6 9.4 %slice-start.3 = ((s8[15728640]{0:T(1024)(128)(4,1)}), s8[3145728]{0:T(1024)(128)(4,1)S(1)}, s32[]{:S(2)}) async-start(s8[15728640]{0:T(1024)(128)(4,1)} %bitcast.33), calls=%async_computation.6 | async-start | bytes 6291456
  139.6 9.4 %collective-permute-start.9 = (bf16[3,3,128,128]{3,2,1,0:T(8,128)(2,1)S(1)}, bf16[3,3,128,128]{3,2,1,0:T(8,128)(2,1)S(1)}, u32[]{:S(2)}, u32[]{:S(2)}) collective-permute-start(bf16[3,3,128,128]{3,2,1,0:T(8,128)(2,1)S(1)} %slice.25), channel_id=1, source_target_pairs={{0,2},{1,3},{2,0},{3,1},{4,6},{5,7},{6,4},{7,5},{8,10},{9,11},{10,... | collective-permute-start | bytes 884744 | tf_op jit(solution)/shard_map/spatial/ppermute | solution.py:418
  153.4 16.2 %collective-permute-start.10 = (bf16[128,2560]{1,0:T(8,128)(2,1)S(1)}, bf16[128,2560]{1,0:T(8,128)(2,1)S(1)}, u32[]{:S(2)}, u32[]{:S(2)}) collective-permute-start(bf16[128,2560]{1,0:T(8,128)(2,1)S(1)} %get-tuple-element.57), channel_id=1, source_target_pairs={{0,1},{1,2},{2,3},{3,0},{4,5},{5,6},{6,7},{7,4},{8,9},{9,10},{10,1... | collective-permute-start | bytes 1966088 | tf_op jit(solution)/shard_map/project/ppermute | solution.py:418
  155.0 14.6 %copy-start.2 = (f32[5120]{0:T(1024)S(1)}, f32[5120]{0:T(1024)}, u32[]{:S(2)}) copy-start(f32[5120]{0:T(1024)} %param.16) | copy-start | bytes 61444
  155.0 14.6 %collective-permute-start.11 = (bf16[128,2560]{1,0:T(8,128)(2,1)S(1)}, bf16[128,2560]{1,0:T(8,128)(2,1)S(1)}, u32[]{:S(2)}, u32[]{:S(2)}) collective-permute-start(bf16[128,2560]{1,0:T(8,128)(2,1)S(1)} %get-tuple-element.58), channel_id=1, source_target_pairs={{0,3},{1,0},{2,1},{3,2},{4,7},{5,4},{6,5},{7,6},{8,11},{9,8},{10,9... | collective-permute-start | bytes 1966088 | tf_op jit(solution)/shard_map/project/ppermute | solution.py:418
Sparse Core Ops, SparseCore 0:
  18.7 87.2 all-gather.2
where the time goes:
time: 178 us
  Pallas kernels  70.9 us (40%)
  waiting for transfers between devices  38.3 us (22%)
  starting transfers between devices  30.1 us (17%)
  blocking collectives  15.9 us (9%)
  between operations  14.2 us (8%)
  local copies, waits for them, and re-layouts  6.45 us (4%)
  other arithmetic  2.03 us (1%)
    ppermute x11, waiting for transfers between devices, along_z(): lax.ppermute(value, 'frm', [(i, (i + shift) % planes) for i in range(plan...  27.3 us
    pallas_call x2, Pallas kernels, heads_both(): pl.pallas_call(lambda *refs: heads_both_kernel(parts, 2 * (buffers is not...  24.8 us
    ppermute x11, starting transfers between devices, along_z(): lax.ppermute(value, 'frm', [(i, (i + shift) % planes) for i in range(plan...  22.9 us
    all_to_all x1, blocking collectives, local(): spatial_out = lax.all_to_all(spatial_out, ('y', 'x'), 0, 0, tiled=True)  15.9 us
    pallas_call x3, Pallas kernels, project(): pl.pallas_call(lambda *refs: project_kernel(targets, groups, *refs), grid...  15.9 us
    pallas_call x2, Pallas kernels, heads(): pl.pallas_call(body, grid=(pairs,), in_specs=in_specs, out_specs=pl.Block...  13.4 us
    pallas_call x1, Pallas kernels, spatial_attention(): pl.pallas_call(spatial_kernel, in_specs=[whole()] * 3, out_specs=whole(),...  11.7 us
    all_to_all x1, waiting for transfers between devices, local(): lax.all_to_all(spatial.reshape(chips, tokens, 3 * HD), ('y', 'x'), 0, 0,...  7.37 us
  transfers between devices with their start and end apart: 14, of which 9 were waited for; matrix products, arithmetic and copies ran while one was open for 2% of the time, Pallas kernels for 30%

commit v1 on v0

--- a/solution.py
+++ b/solution.py
@@ -183,7 +183,7 @@
     )(*args)
 
 
-def spatial_kernel(own_ref, other_ref, bias_ref, out_ref):
+def spatial_kernel(side, own_ref, keys_ref, bias_ref, *refs):
     blocks = own_ref.shape[0]
     rows = blocks * BLK
     shape = (blocks, BLK, HD)
@@ -193,8 +193,9 @@
     per_chunk = 4
     chunk = per_chunk * BLK
     ones = jnp.ones((chunk, HD), jnp.bfloat16)
-    summed = jnp.zeros((rows, 2 * HD), jnp.float32)
-    for side, ref in enumerate((own_ref, other_ref)):
+    out_ref = refs[-1]
+    summed = jnp.zeros((rows, 2 * HD), jnp.float32) if side == 0 else refs[0][...]
+    for ref in (keys_ref,):
         for at in range(0, blocks, per_chunk):
             row = side * blocks + at
             bias = jnp.concatenate(
@@ -214,23 +215,27 @@
                 jnp.exp2(scores).astype(jnp.bfloat16), jnp.concatenate([values, ones], axis=1),
                 preferred_element_type=jnp.float32,
             )
+    if side == 0:
+        out_ref[...] = summed
+        return
     out_ref[...] = (summed[:, :HD] / summed[:, HD:]).astype(jnp.bfloat16).reshape(shape)
 
 
-def spatial_attention(own, other, bias):
+def spatial_attention(own, keys, bias, partial=None):
     blocks, tokens, triple = own.shape
-    total = 2 * blocks * tokens
-    return pl.pallas_call(
-        spatial_kernel,
-        in_specs=[whole()] * 3,
+    rows = blocks * tokens
+    side = 0 if partial is None else 1
+    args = [own, keys, bias] + ([] if partial is None else [partial])
+    out = ((rows, 2 * HD), jnp.float32) if side == 0 else ((blocks, tokens, HD), jnp.bfloat16)
+    return pl.pallas_call(
+        lambda *refs: spatial_kernel(side, *refs),
+        in_specs=[whole()] * len(args),
         out_specs=whole(),
-        out_shape=jax.ShapeDtypeStruct((blocks, tokens, HD), jnp.bfloat16),
+        out_shape=jax.ShapeDtypeStruct(*out),
         compiler_params=params(),
-        cost_estimate=cost(
-            8 * blocks * tokens * total * HD, 4 * blocks * tokens * triple, blocks * tokens * total
-        ),
-        name="spatial_attention",
-    )(own, other, bias)
+        cost_estimate=cost(8 * rows * rows * HD, 4 * rows * triple, rows * rows),
+        name=("spatial_attention_own", "spatial_attention_other")[side],
+    )(*args)
 
 
 def temporal_kernel(qkv_ref, bias_ref, out_ref):
@@ -487,7 +492,8 @@
             (mine, temporal_out, temporal_far, bias_s, out_weight)
         )
         other = swap_cores(mine)
-        spatial_out = spatial_attention(mine, other, bias_s)
+        partial = spatial_attention(mine, mine, bias_s)
+        spatial_out = spatial_attention(mine, other, bias_s, partial)
         spatial_out = lax.all_to_all(spatial_out, ("y", "x"), 0, 0, tiled=True)
         spatial_out = spatial_out.reshape(4, 4, tokens, HD)
         spatial_far = along_z(spatial_out[1:, :pairs], 2)

time: 178 us -> 178 us (level)
  waiting for transfers between devices: 38.3 us -> 34.7 us
  Pallas kernels: 70.9 us -> 73.2 us
    ppermute x1, waiting for transfers between devices: 3.62 us -> 0.01 us  [swap_cores(): return lax.ppermute(value, 'core', [(0, 1), (1, 0)])]
    pallas_call x1 -> x2, Pallas kernels: 11.7 us -> 14 us  [spatial_attention(): pl.pallas_call(lambda *refs: spatial_kernel(side, *refs), in_specs=[whole...]
  transfers between devices with their start and end apart: 14 -> 14, of which waited for: 9 -> 8; matrix products, arithmetic and copies ran while one was open for 2% -> 2% of each run, Pallas kernels for 30% -> 35%
where the time goes in v1:
time: 178 us; the launch traced here: 177 us
  Pallas kernels  73.2 us (41%)
  waiting for transfers between devices  34.7 us (19%)
  starting transfers between devices  30.3 us (17%)
  blocking collectives  16.1 us (9%)
  between operations  14.3 us (8%)
  local copies, waits for them, and re-layouts  6.45 us (4%)
  other arithmetic  2.03 us (1%)
    ppermute x11, waiting for transfers between devices, along_z(): lax.ppermute(value, 'frm', [(i, (i + shift) % planes) for i in range(plan...  27.3 us
    pallas_call x2, Pallas kernels, heads_both(): pl.pallas_call(lambda *refs: heads_both_kernel(parts, 2 * (buffers is not...  24.8 us
    ppermute x11, starting transfers between devices, along_z(): lax.ppermute(value, 'frm', [(i, (i + shift) % planes) for i in range(plan...  23.1 us
    all_to_all x1, blocking collectives, local(): spatial_out = lax.all_to_all(spatial_out, ('y', 'x'), 0, 0, tiled=True)  16.1 us
    pallas_call x3, Pallas kernels, project(): pl.pallas_call(lambda *refs: project_kernel(targets, groups, *refs), grid...  15.9 us
    pallas_call x2, Pallas kernels, spatial_attention(): pl.pallas_call(lambda *refs: spatial_kernel(side, *refs), in_specs=[whole...  14 us
    pallas_call x2, Pallas kernels, heads(): pl.pallas_call(body, grid=(pairs,), in_specs=in_specs, out_specs=pl.Block...  13.4 us
    all_to_all x1, waiting for transfers between devices, local(): lax.all_to_all(spatial.reshape(chips, tokens, 3 * HD), ('y', 'x'), 0, 0,...  7.37 us
  transfers between devices with their start and end apart: 14, of which 8 were waited for; matrix products, arithmetic and copies ran while one was open for 2% of the time, Pallas kernels for 35%

profile of v1, /device:TPU:0, one launch (start us, length us, event | category | flops | bytes accessed | tf_op | source)
XLA Modules:
  0.0 177.0 jit_solution(14295828044381523330)
XLA Ops:
  6.5 4.0 %collective-permute-start = (bf16[3,2,160,128]{3,2,1,0:T(8,128)(2,1)}, bf16[3,2,160,128]{3,2,1,0:T(8,128)(2,1)S(1)}, u32[]{:S(2)}, u32[]{:S(2)}) collective-permute-start(bf16[3,2,160,128]{3,2,1,0:T(8,128)(2,1)} %bitcast.49), channel_id=1, source_target_pairs={{0,2},{1,3},{2,0},{3,1},{4,6},{5,7},{6,4},{7,5},{8,10},{9,11},{10,... | collective-permute-start | bytes 737288 | tf_op jit(solution)/shard_map/gather_w_out/ppermute | solution.py:423
  10.6 1.3 copy-done.1
  11.9 0.7 copy-done.3
  12.6 0.7 copy-done.4
  13.4 1.8 %modulate.1 = (bf16[64,5120]{1,0:T(8,128)(2,1)}, bf16[64,5120]{1,0:T(8,128)(2,1)S(1)}) custom-call(bf16[128,5120]{1,0:T(8,128)(2,1)S(1)} %bitcast.40, f32[1,5120]{1,0:T(1,128)S(1)} %bitcast.43, f32[1,5120]{1,0:T(1,128)S(1)} %bitcast.44), custom_call_target="tpu_custom_call" | custom-call | flops 6553600 | bytes 2621440 | tf_op jit(solution)/shard_map/modulate/modulate/pallas_call | solution.py:46
  15.2 1.6 collective-permute-done
  16.8 1.8 pad_maximum_fusion
  18.5 1.4 collective-permute-start.1
  19.9 2.2 %collective-permute-start.2 = (bf16[64,5120]{1,0:T(8,128)(2,1)S(1)}, bf16[64,5120]{1,0:T(8,128)(2,1)}, u32[]{:S(2)}, u32[]{:S(2)}) collective-permute-start(bf16[64,5120]{1,0:T(8,128)(2,1)S(1)} %get-tuple-element.35.refs_1_), channel_id=1, source_target_pairs={{0,3},{1,0},{2,1},{3,2},{4,7},{5,4},{6,5},{7,6},{8,11},{9,8},{10,9... | collective-permute-start | bytes 1966088 | tf_op jit(solution)/shard_map/qkv/ppermute | solution.py:423
  22.1 1.9 %collective-permute-start.5 = (bf16[64,5120]{1,0:T(8,128)(2,1)}, bf16[64,5120]{1,0:T(8,128)(2,1)}, u32[]{:S(2)}, u32[]{:S(2)}) collective-permute-start(bf16[64,5120]{1,0:T(8,128)(2,1)} %get-tuple-element.34.refs_0_), channel_id=1, source_target_pairs={{0,3},{1,0},{2,1},{3,2},{4,7},{5,4},{6,5},{7,6},{8,11},{9,8},{10,9... | collective-permute-start | bytes 1966088 | tf_op jit(solution)/shard_map/qkv/ppermute | solution.py:423
  24.0 0.1 collective-permute-start.6
  24.2 10.5 %qkv_both.2 = (bf16[4,4,128,384]{3,2,1,0:T(8,128)(2,1)}, bf16[4,3,128,384]{3,2,1,0:T(8,128)(2,1)S(1)}) custom-call(bf16[64,5120]{1,0:T(8,128)(2,1)} %get-tuple-element.34.refs_0_, bf16[64,5120]{1,0:T(8,128)(2,1)S(1)} %get-tuple-element.35.refs_1_, bf16[3,6,5120,128]{3,2,1,0:T(8,128)(2,1)} %bitcast.45, f32[2,3,2,128]{3,2,1,0:T(2,128)S(1)} %fusion.refs_3_.refs_5_), custom_call_target="tpu_custom_call" | custom-call | flops 3019898880 | bytes 23592960 | tf_op jit(solution)/shard_map/qkv/qkv_both/pallas_call | solution.py:132
  34.7 3.2 %collective-permute-done.1.refs_2_ = bf16[64,5120]{1,0:T(8,128)(2,1)} collective-permute-done((bf16[64,5120]{1,0:T(8,128)(2,1)}, bf16[64,5120]{1,0:T(8,128)(2,1)}, u32[]{:S(2)}, u32[]{:S(2)}) %collective-permute-start.1) | collective-permute-done | bytes 655392 | tf_op jit(solution)/shard_map/qkv/ppermute | solution.py:423
  38.0 1.6 collective-permute-start.3
  39.6 1.6 collective-permute-start.4
  41.2 10.5 %collective-permute-done.5.refs_0_ = bf16[64,5120]{1,0:T(8,128)(2,1)} collective-permute-done((bf16[64,5120]{1,0:T(8,128)(2,1)}, bf16[64,5120]{1,0:T(8,128)(2,1)}, u32[]{:S(2)}, u32[]{:S(2)}) %collective-permute-start.5) | collective-permute-done | bytes 655392 | tf_op jit(solution)/shard_map/qkv/ppermute | solution.py:423
  51.7 0.3 collective-permute-done.6.refs_3_
  52.0 14.3 %qkv_both.3 = (bf16[4,4,128,384]{3,2,1,0:T(8,128)(2,1)}, bf16[4,3,128,384]{3,2,1,0:T(8,128)(2,1)S(1)}) custom-call(bf16[64,5120]{1,0:T(8,128)(2,1)} %collective-permute-done.5.refs_0_, bf16[64,5120]{1,0:T(8,128)(2,1)} %collective-permute-done.2.refs_1_, ...), custom_call_target="tpu_custom_call", output_to_operand_aliasing={{0}: (6, {}), {1}: (7, {})} | custom-call | flops 6039797760 | bytes 23592960 | tf_op jit(solution)/shard_map/qkv/qkv_both/pallas_call | solution.py:132
  66.3 7.2 %qkv_spatial.1 = bf16[4,4,128,384]{3,2,1,0:T(8,128)(2,1)} custom-call(bf16[64,5120]{1,0:T(8,128)(2,1)S(1)} %collective-permute-done.3.refs_0_, bf16[64,5120]{1,0:T(8,128)(2,1)S(1)} %collective-permute-done.4.refs_1_, bf16[3,6,5120,128]{3,2,1,0:T(8,128)(2,1)} %bitcast.47, f32[3,2,128]{2,1,0:T(2,128)S(1)} %get-tuple-element.62.refs_3_, ...), custom_call_target="tpu_custom_call", output_to_operand_aliasing={{}: (4, {})} | custom-call | flops 1509949440 | bytes 11796480 | tf_op jit(solution)/shard_map/qkv/qkv_spatial/pallas_call | solution.py:172
  73.5 7.2 %all-to-all-start = ((bf16[16,128,384]{2,1,0:T(8,128)(2,1)}), bf16[16,128,384]{2,1,0:T(8,128)(2,1)}, u32[]{:S(2)}, u32[]{:S(2)}) async-start(bf16[16,128,384]{2,1,0:T(8,128)(2,1)} %bitcast.8), calls=%async_computation | async-start | bytes 3145728 | tf_op jit(solution)/shard_map/spatial/all_to_all | solution.py:488
  80.8 0.6 dynamic_slice.23
  82.1 0.2 copy.30
  82.3 0.6 gather_fusion
  82.9 0.1 copy.26
  83.0 0.6 gather_fusion.1
  83.6 0.6 gather_fusion.2
  84.4 0.1 copy.27
  84.5 6.2 %qkv_temporal.1.qkv_ref = bf16[4,3,128,384]{3,2,1,0:T(8,128)(2,1)S(1)} custom-call(bf16[64,5120]{1,0:T(8,128)(2,1)S(1)} %collective-permute-done.3.refs_0_, bf16[64,5120]{1,0:T(8,128)(2,1)S(1)} %collective-permute-done.4.refs_1_, bf16[3,6,5120,128]{3,2,1,0:T(8,128)(2,1)} %bitcast.48, ...), custom_call_target="tpu_custom_call", output_to_operand_aliasing={{}: (4, {})} | custom-call | flops 1509949440 | bytes 11796480 | tf_op jit(solution)/shard_map/qkv/qkv_temporal/pallas_call | solution.py:172
  90.8 1.9 %temporal_attention.1.refs_1_ = bf16[4,3,128,128]{3,2,1,0:T(8,128)(2,1)S(1)} custom-call(bf16[4,3,128,384]{3,2,1,0:T(8,128)(2,1)S(1)} %qkv_temporal.1.qkv_ref, f32[3,4,1,512]{3,2,1,0:T(1,128)S(1)} %bitcast.41), custom_call_target="tpu_custom_call" | custom-call | flops 603979776 | bytes 1179648 | tf_op jit(solution)/shard_map/temporal/temporal_attention/pallas_call | solution.py:261
  92.7 3.5 %collective-permute-start.7 = (bf16[3,3,128,128]{3,2,1,0:T(8,128)(2,1)S(1)}, bf16[3,3,128,128]{3,2,1,0:T(8,128)(2,1)S(1)}, u32[]{:S(2)}, u32[]{:S(2)}) collective-permute-start(bf16[3,3,128,128]{3,2,1,0:T(8,128)(2,1)S(1)} %slice.24), channel_id=1, source_target_pairs={{0,2},{1,3},{2,0},{3,1},{4,6},{5,7},{6,4},{7,5},{8,10},{9,11},{10,... | collective-permute-start | bytes 884744 | tf_op jit(solution)/shard_map/temporal/ppermute | solution.py:423
  96.2 0.2 reshape.65
  96.3 0.1 constant_dynamic-slice_fusion.1
  96.5 0.2 copy.28
  96.7 0.2 copy.29
  96.9 4.1 %collective-permute-done.7.refs_3_.refs_1_ = bf16[3,3,128,128]{3,2,1,0:T(8,128)(2,1)S(1)} collective-permute-done((bf16[3,3,128,128]{3,2,1,0:T(8,128)(2,1)S(1)}, bf16[3,3,128,128]{3,2,1,0:T(8,128)(2,1)S(1)}, u32[]{:S(2)}, u32[]{:S(2)}) %collective-permute-start.7) | collective-permute-done | bytes 294944 | tf_op jit(solution)/shard_map/temporal/ppermute | solution.py:423
  101.0 7.4 %all-to-all-done.refs_0_.refs_1_ = bf16[16,128,384]{2,1,0:T(8,128)(2,1)} async-done(((bf16[16,128,384]{2,1,0:T(8,128)(2,1)}), bf16[16,128,384]{2,1,0:T(8,128)(2,1)}, u32[]{:S(2)}, u32[]{:S(2)}) %all-to-all-start) | async-done | bytes 1572896 | tf_op jit(solution)/shard_map/spatial/all_to_all | solution.py:488
  108.4 7.7 %spatial_attention_own.1.refs_3_ = f32[2048,256]{1,0:T(8,128)S(1)} custom-call(bf16[16,128,384]{2,1,0:T(8,128)(2,1)} %all-to-all-done.refs_0_.refs_1_, bf16[16,128,384]{2,1,0:T(8,128)(2,1)} %all-to-all-done.refs_0_.refs_1_, f32[32,128]{1,0:T(8,128)S(1)} %pad.4.refs_2_), custom_call_target="tpu_custom_call" | custom-call | flops 4294967296 | bytes 3145728 | tf_op jit(solution)/shard_map/spatial/spatial_attention_own/pallas_call | solution.py:230
  116.1 6.2 %spatial_attention_other.1 = bf16[16,128,128]{2,1,0:T(8,128)(2,1)S(1)} custom-call(bf16[16,128,384]{2,1,0:T(8,128)(2,1)} %all-to-all-done.refs_0_.refs_1_, bf16[16,128,384]{2,1,0:T(8,128)(2,1)S(1)} %collective-permute-done.8.refs_1_, f32[32,128]{1,0:T(8,128)S(1)} %pad.4.refs_2_, f32[2048,256]{1,0:T(8,128)S(1)} %spatial_attention_own.1.refs_3_), custom_call_target="tpu_custom_call" | custom-call | flops 4294967296 | bytes 3145728 | tf_op jit(solution)/shard_map/spatial/spatial_attention_other/pallas_call | solution.py:230
  122.4 16.1 %all_to_all.10 = bf16[16,128,128]{2,1,0:T(8,128)(2,1)S(1)} all-to-all(bf16[16,128,128]{2,1,0:T(8,128)(2,1)S(1)} %spatial_attention_other.1), channel_id=1, replica_groups=mesh['y'=4,'x'=4,'core'=2,'frm'=4] {'y','x'}, dimensions={0} | all-to-all | bytes 1048576 | tf_op jit(solution)/shard_map/spatial/all_to_all | solution.py:497
  138.6 3.4 %collective-permute-start.9 = (bf16[3,3,128,128]{3,2,1,0:T(8,128)(2,1)S(1)}, bf16[3,3,128,128]{3,2,1,0:T(8,128)(2,1)S(1)}, u32[]{:S(2)}, u32[]{:S(2)}) collective-permute-start(bf16[3,3,128,128]{3,2,1,0:T(8,128)(2,1)S(1)} %slice.25), channel_id=1, source_target_pairs={{0,2},{1,3},{2,0},{3,1},{4,6},{5,7},{6,4},{7,5},{8,10},{9,11},{10,... | collective-permute-start | bytes 884744 | tf_op jit(solution)/shard_map/spatial/ppermute | solution.py:423
  142.0 5.9 %project_sent_own_group.1.refs_3_ = f32[128,5120]{1,0:T(8,128)S(1)} custom-call(bf16[4,4,128,128]{3,2,1,0:T(8,128)(2,1)S(1)} %bitcast.38, bf16[4,3,128,128]{3,2,1,0:T(8,128)(2,1)S(1)} %temporal_attention.1.refs_1_, bf16[32,2,3,2,160,128]{5,4,3,2,1,0:T(8,128)(2,1)} %bitcast.32), custom_call_target="tpu_custom_call" | custom-call | flops 1006632960 | bytes 7864320 | tf_op jit(solution)/shard_map/project/project_sent_own_group/pallas_call | solution.py:344
  147.9 0.3 collective-permute-done.9.refs_2_.refs_0_
  148.2 4.3 %project_sent.1 = (bf16[128,2560]{1,0:T(8,128)(2,1)S(1)}, bf16[128,2560]{1,0:T(8,128)(2,1)S(1)}) custom-call(bf16[3,3,128,128]{3,2,1,0:T(8,128)(2,1)S(1)} %collective-permute-done.9.refs_2_.refs_0_, bf16[3,3,128,128]{3,2,1,0:T(8,128)(2,1)S(1)} %collective-permute-done.7.refs_3_.refs_1_, bf16[32,2,3,2,160,128]{5,4,3,2,1,0:T(8,128)(2,1)S(1)} %bitcast.35, ...), custom_call_target="tpu_custom_call" | custom-call | flops 1006632960 | bytes 7864320 | tf_op jit(solution)/shard_map/project/project_sent/pallas_call | solution.py:344
  152.5 1.6 collective-permute-start.10
  154.1 1.7 collective-permute-start.11
  155.8 5.7 %project_kept.1.own_ref = bf16[128,5120]{1,0:T(8,128)(2,1)S(1)} custom-call(bf16[4,4,128,128]{3,2,1,0:T(8,128)(2,1)S(1)} %bitcast.39, bf16[4,3,128,128]{3,2,1,0:T(8,128)(2,1)S(1)} %temporal_attention.1.refs_1_, bf16[3,3,128,128]{3,2,1,0:T(8,128)(2,1)S(1)} %collective-permute-done.9.refs_2_.refs_0_, ...), custom_call_target="tpu_custom_call" | custom-call | flops 2013265920 | bytes 15728640 | tf_op jit(solution)/shard_map/project/project_kept/pallas_call | solution.py:344
  161.5 7.2 %collective-permute-done.10.low_ref = bf16[128,2560]{1,0:T(8,128)(2,1)S(1)} collective-permute-done((bf16[128,2560]{1,0:T(8,128)(2,1)S(1)}, bf16[128,2560]{1,0:T(8,128)(2,1)S(1)}, u32[]{:S(2)}, u32[]{:S(2)}) %collective-permute-start.10) | collective-permute-done | bytes 655392 | tf_op jit(solution)/shard_map/project/ppermute | solution.py:423
  168.8 1.4 combine.1
  (50 shorter events, 0.6 us)
Async XLA Ops:
  6.5 89.6 %copy-start = (s32[3,4,32,32]{3,2,1,0:T(8,128)S(1)}, s32[3,4,32,32]{3,2,1,0:T(8,128)}, u32[]{:S(2)}) copy-start(s32[3,4,32,32]{3,2,1,0:T(8,128)} %param.20) | copy-start | bytes 147460
  6.5 17.6 %copy-start.7 = (f32[2]{0:T(128)S(1)}, f32[2]{0:T(128)}, u32[]{:S(2)}) copy-start(f32[2]{0:T(128)} %constant.151.clone) | copy-start | bytes 28
  6.5 17.6 %copy-start.6 = (f32[3,4,128]{2,1,0:T(4,128)S(1)}, f32[3,4,128]{2,1,0:T(4,128)}, u32[]{:S(2)}) copy-start(f32[3,4,128]{2,1,0:T(4,128)} %param.18) | copy-start | bytes 18436
  6.5 101.8 %all-gather.3.cloned.1.call-start = ((), (), s32[]{:S(2)}) async-start(), calls=%async_computation.2 | async-start | bytes 16220160 | tf_op jit(solution)/shard_map/gather_w_out/all_gather | solution.py:435
  6.5 10.2 %collective-permute-start = (bf16[3,2,160,128]{3,2,1,0:T(8,128)(2,1)}, bf16[3,2,160,128]{3,2,1,0:T(8,128)(2,1)S(1)}, u32[]{:S(2)}, u32[]{:S(2)}) collective-permute-start(bf16[3,2,160,128]{3,2,1,0:T(8,128)(2,1)} %bitcast.49), channel_id=1, source_target_pairs={{0,2},{1,3},{2,0},{3,1},{4,6},{5,7},{6,4},{7,5},{8,10},{9,11},{10,... | collective-permute-start | bytes 737288 | tf_op jit(solution)/shard_map/gather_w_out/ppermute | solution.py:423
  10.6 1.3 copy-start.1
  11.9 0.7 copy-start.3
  12.6 0.7 copy-start.4
  18.5 19.4 %collective-permute-start.1 = (bf16[64,5120]{1,0:T(8,128)(2,1)}, bf16[64,5120]{1,0:T(8,128)(2,1)}, u32[]{:S(2)}, u32[]{:S(2)}) collective-permute-start(bf16[64,5120]{1,0:T(8,128)(2,1)} %get-tuple-element.34.refs_0_), channel_id=1, source_target_pairs={{0,1},{1,2},{2,3},{3,0},{4,5},{5,6},{6,7},{7,4},{8,9},{9,10},{10,1... | collective-permute-start | bytes 1966088 | tf_op jit(solution)/shard_map/qkv/ppermute | solution.py:423
  19.9 18.1 %collective-permute-start.2 = (bf16[64,5120]{1,0:T(8,128)(2,1)S(1)}, bf16[64,5120]{1,0:T(8,128)(2,1)}, u32[]{:S(2)}, u32[]{:S(2)}) collective-permute-start(bf16[64,5120]{1,0:T(8,128)(2,1)S(1)} %get-tuple-element.35.refs_1_), channel_id=1, source_target_pairs={{0,3},{1,0},{2,1},{3,2},{4,7},{5,4},{6,5},{7,6},{8,11},{9,8},{10,9... | collective-permute-start | bytes 1966088 | tf_op jit(solution)/shard_map/qkv/ppermute | solution.py:423
  22.1 29.6 %collective-permute-start.5 = (bf16[64,5120]{1,0:T(8,128)(2,1)}, bf16[64,5120]{1,0:T(8,128)(2,1)}, u32[]{:S(2)}, u32[]{:S(2)}) collective-permute-start(bf16[64,5120]{1,0:T(8,128)(2,1)} %get-tuple-element.34.refs_0_), channel_id=1, source_target_pairs={{0,3},{1,0},{2,1},{3,2},{4,7},{5,4},{6,5},{7,6},{8,11},{9,8},{10,9... | collective-permute-start | bytes 1966088 | tf_op jit(solution)/shard_map/qkv/ppermute | solution.py:423
  24.0 28.0 %collective-permute-start.6 = (bf16[64,5120]{1,0:T(8,128)(2,1)S(1)}, bf16[64,5120]{1,0:T(8,128)(2,1)}, u32[]{:S(2)}, u32[]{:S(2)}) collective-permute-start(bf16[64,5120]{1,0:T(8,128)(2,1)S(1)} %get-tuple-element.35.refs_1_), channel_id=1, source_target_pairs={{0,1},{1,2},{2,3},{3,0},{4,5},{5,6},{6,7},{7,4},{8,9},{9,10},{10,1... | collective-permute-start | bytes 1966088 | tf_op jit(solution)/shard_map/qkv/ppermute | solution.py:423
  38.0 28.4 %collective-permute-start.3 = (bf16[64,5120]{1,0:T(8,128)(2,1)}, bf16[64,5120]{1,0:T(8,128)(2,1)S(1)}, u32[]{:S(2)}, u32[]{:S(2)}) collective-permute-start(bf16[64,5120]{1,0:T(8,128)(2,1)} %collective-permute-done.1.refs_2_), channel_id=1, source_target_pairs={{0,1},{1,2},{2,3},{3,0},{4,5},{5,6},{6,7},{7,4},{8,9},{9,10},{10,1... | collective-permute-start | bytes 1966088 | tf_op jit(solution)/shard_map/qkv/ppermute | solution.py:423
  39.6 26.8 %collective-permute-start.4 = (bf16[64,5120]{1,0:T(8,128)(2,1)}, bf16[64,5120]{1,0:T(8,128)(2,1)S(1)}, u32[]{:S(2)}, u32[]{:S(2)}) collective-permute-start(bf16[64,5120]{1,0:T(8,128)(2,1)} %collective-permute-done.2.refs_1_), channel_id=1, source_target_pairs={{0,3},{1,0},{2,1},{3,2},{4,7},{5,4},{6,5},{7,6},{8,11},{9,8},{10,9... | collective-permute-start | bytes 1966088 | tf_op jit(solution)/shard_map/qkv/ppermute | solution.py:423
  73.5 7.2 %copy-start.5 = (s32[3,32,4,4]{1,3,2,0:T(4,128)S(1)}, s32[3,32,4,4]{1,3,2,0:T(4,128)}, u32[]{:S(2)}) copy-start(s32[3,32,4,4]{1,3,2,0:T(4,128)} %param.21) | copy-start | bytes 18436
  73.5 7.3 %copy-start.9 = (s32[4]{0:T(128)S(1)}, s32[4]{0:T(128)}, u32[]{:S(2)}) copy-start(s32[4]{0:T(128)} %constant.152.clone) | copy-start | bytes 52
  73.5 10.0 %copy-start.8 = (s32[4]{0:T(128)S(1)}, s32[4]{0:T(128)}, u32[]{:S(2)}) copy-start(s32[4]{0:T(128)} %param.22) | copy-start | bytes 52
  73.5 34.9 %all-to-all-start = ((bf16[16,128,384]{2,1,0:T(8,128)(2,1)}), bf16[16,128,384]{2,1,0:T(8,128)(2,1)}, u32[]{:S(2)}, u32[]{:S(2)}) async-start(bf16[16,128,384]{2,1,0:T(8,128)(2,1)} %bitcast.8), calls=%async_computation | async-start | bytes 3145728 | tf_op jit(solution)/shard_map/spatial/all_to_all | solution.py:488
  92.7 8.3 %collective-permute-start.7 = (bf16[3,3,128,128]{3,2,1,0:T(8,128)(2,1)S(1)}, bf16[3,3,128,128]{3,2,1,0:T(8,128)(2,1)S(1)}, u32[]{:S(2)}, u32[]{:S(2)}) collective-permute-start(bf16[3,3,128,128]{3,2,1,0:T(8,128)(2,1)S(1)} %slice.24), channel_id=1, source_target_pairs={{0,2},{1,3},{2,0},{3,1},{4,6},{5,7},{6,4},{7,5},{8,10},{9,11},{10,... | collective-permute-start | bytes 884744 | tf_op jit(solution)/shard_map/temporal/ppermute | solution.py:423
  108.4 7.7 %collective-permute-start.8 = (bf16[16,128,384]{2,1,0:T(8,128)(2,1)}, bf16[16,128,384]{2,1,0:T(8,128)(2,1)S(1)}, u32[]{:S(2)}, u32[]{:S(2)}) collective-permute-start(bf16[16,128,384]{2,1,0:T(8,128)(2,1)} %all-to-all-done.refs_0_.refs_1_), channel_id=1, source_target_pairs={{0,4},{4,0},{1,5},{5,1},{2,6},{6,2},{3,7},{7,3},{8,12},{12,8},{9,1... | collective-permute-start | bytes 4718600 | tf_op jit(solution)/shard_map/spatial/ppermute | solution.py:426
  116.1 32.0 %slice-start = ((s8[15728640]{0:T(1024)(128)(4,1)}), s8[4194304]{0:T(1024)(128)(4,1)S(1)}, s32[]{:S(2)}) async-start(s8[15728640]{0:T(1024)(128)(4,1)} %bitcast.33), calls=%async_computation.3 | async-start | bytes 8388608
  116.1 32.0 %slice-start.1 = ((s8[15728640]{0:T(1024)(128)(4,1)}), s8[4194304]{0:T(1024)(128)(4,1)S(1)}, s32[]{:S(2)}) async-start(s8[15728640]{0:T(1024)(128)(4,1)} %bitcast.33), calls=%async_computation.4 | async-start | bytes 8388608
  138.5 9.6 %slice-start.2 = ((s8[15728640]{0:T(1024)(128)(4,1)}), s8[4194304]{0:T(1024)(128)(4,1)S(1)}, s32[]{:S(2)}) async-start(s8[15728640]{0:T(1024)(128)(4,1)} %bitcast.33), calls=%async_computation.5 | async-start | bytes 8388608
  138.6 9.6 %slice-start.3 = ((s8[15728640]{0:T(1024)(128)(4,1)}), s8[3145728]{0:T(1024)(128)(4,1)S(1)}, s32[]{:S(2)}) async-start(s8[15728640]{0:T(1024)(128)(4,1)} %bitcast.33), calls=%async_computation.6 | async-start | bytes 6291456
  138.6 9.6 %collective-permute-start.9 = (bf16[3,3,128,128]{3,2,1,0:T(8,128)(2,1)S(1)}, bf16[3,3,128,128]{3,2,1,0:T(8,128)(2,1)S(1)}, u32[]{:S(2)}, u32[]{:S(2)}) collective-permute-start(bf16[3,3,128,128]{3,2,1,0:T(8,128)(2,1)S(1)} %slice.25), channel_id=1, source_target_pairs={{0,2},{1,3},{2,0},{3,1},{4,6},{5,7},{6,4},{7,5},{8,10},{9,11},{10,... | collective-permute-start | bytes 884744 | tf_op jit(solution)/shard_map/spatial/ppermute | solution.py:423
  152.5 16.2 %collective-permute-start.10 = (bf16[128,2560]{1,0:T(8,128)(2,1)S(1)}, bf16[128,2560]{1,0:T(8,128)(2,1)S(1)}, u32[]{:S(2)}, u32[]{:S(2)}) collective-permute-start(bf16[128,2560]{1,0:T(8,128)(2,1)S(1)} %get-tuple-element.57), channel_id=1, source_target_pairs={{0,1},{1,2},{2,3},{3,0},{4,5},{5,6},{6,7},{7,4},{8,9},{9,10},{10,1... | collective-permute-start | bytes 1966088 | tf_op jit(solution)/shard_map/project/ppermute | solution.py:423
  154.1 14.6 %copy-start.2 = (f32[5120]{0:T(1024)S(1)}, f32[5120]{0:T(1024)}, u32[]{:S(2)}) copy-start(f32[5120]{0:T(1024)} %param.16) | copy-start | bytes 61444
  154.1 14.6 %collective-permute-start.11 = (bf16[128,2560]{1,0:T(8,128)(2,1)S(1)}, bf16[128,2560]{1,0:T(8,128)(2,1)S(1)}, u32[]{:S(2)}, u32[]{:S(2)}) collective-permute-start(bf16[128,2560]{1,0:T(8,128)(2,1)S(1)} %get-tuple-element.58), channel_id=1, source_target_pairs={{0,3},{1,0},{2,1},{3,2},{4,7},{5,4},{6,5},{7,6},{8,11},{9,8},{10,9... | collective-permute-start | bytes 1966088 | tf_op jit(solution)/shard_map/project/ppermute | solution.py:423
Sparse Core Ops, SparseCore 0:
  18.7 87.2 all-gather.2

commit v2 on v1

--- a/solution.py
+++ b/solution.py
@@ -277,8 +277,8 @@
 FAR_SLOT = {0: 0, 1: 2, -1: 1}
 
 
-def project_kernel(targets, groups, *refs):
-    heads_count = 2 * len(groups)
+def project_kernel(targets, groups, used, has_partial, *refs):
+    heads_count = len(used) * len(groups)
     head_refs, w_ref = refs[:heads_count], refs[heads_count]
     rest, rows_ref = refs[heads_count + 1 : -1], refs[-1]
     step, steps = pl.program_id(0), pl.num_programs(0)
@@ -291,7 +291,7 @@
             for at_group, group in enumerate(groups):
                 slot = (OWN_SLOT, FAR_SLOT)[group][target]
                 for kind in range(kinds):
-                    ref = head_refs[2 * at_group + kind]
+                    ref = head_refs[len(used) * at_group + kind]
                     for pair in range(pairs):
                         at = at_group * depth + (pair * kinds + kind) * HD
                         rows_ref[number, :, at : at + HD] = ref[slot, pair]
@@ -309,11 +309,14 @@
     product = lax.dot_general(
         rows, weight, (((1,), (1,)), ((), ())), preferred_element_type=jnp.float32
     )
+    if has_partial:
+        product = product + rest[0][...]
+        rest = rest[1:]
+    product = product.astype(rest[0].dtype)
     if len(rest) == 1:
-        rest[0][...] = product.astype(rest[0].dtype)
+        rest[0][...] = product
         return
-    partial_ref, low_ref, high_ref = rest
-    product = (product + partial_ref[...]).astype(jnp.bfloat16)
+    low_ref, high_ref = rest
 
     @pl.when(step < steps // 2)
     def _():
@@ -324,15 +327,19 @@
         high_ref[...] = product
 
 
-def project(name, targets, groups, head_arrays, weight, dtype, limit, partial=None):
-    shards, _, pairs, kinds, shard, _ = weight.shape
+def project(
+    name, targets, groups, used, head_arrays, weight, dtype, limit, partial=None, split=False
+):
+    shards, _, pairs, _, shard, _ = weight.shape
+    kinds = len(used)
     per_step = 8
     steps, width = shards // per_step, per_step * shard
     depth = len(groups) * kinds * pairs * HD
     first = groups[0] // len(groups)
+    first_kind = used[0] // kinds
     column = pl.BlockSpec((BLK, width), lambda n: (0, n))
     partials = [] if partial is None else [partial]
-    if partial is None:
+    if not split:
         out_specs = column
         out_shape = jax.ShapeDtypeStruct((BLK, steps * width), dtype)
     else:
@@ -342,13 +349,13 @@
         ]
         out_shape = [jax.ShapeDtypeStruct((BLK, steps // 2 * width), dtype)] * 2
     return pl.pallas_call(
-        lambda *refs: project_kernel(targets, groups, *refs),
+        lambda *refs: project_kernel(targets, groups, used, partial is not None, *refs),
         grid=(steps,),
         in_specs=[pl.BlockSpec(array.shape, lambda n: (0, 0, 0, 0)) for array in head_arrays]
         + [
             pl.BlockSpec(
                 (per_step, len(groups), pairs, kinds, shard, HD),
-                lambda n: (n, first, 0, 0, 0, 0),
+                lambda n: (n, first, 0, first_kind, 0, 0),
             )
         ]
         + [column] * len(partials),
@@ -491,6 +498,10 @@
         mine, temporal_out, temporal_far, bias_s, out_weight = lax.optimization_barrier(
             (mine, temporal_out, temporal_far, bias_s, out_weight)
         )
+        sent = project(
+            "project_sent_temporal",
+            (1, -1), (0, 1), (1,), [temporal_out, temporal_far], out_weight, jnp.float32, WIDE,
+        )
         other = swap_cores(mine)
         partial = spatial_attention(mine, mine, bias_s)
         spatial_out = spatial_attention(mine, other, bias_s, partial)
@@ -499,17 +510,19 @@
         spatial_far = along_z(spatial_out[1:, :pairs], 2)
 
     with jax.named_scope("project"):
-        own_heads, far_heads = [spatial_out, temporal_out], [spatial_far, temporal_far]
         sent = project(
-            "project_sent_own_group", (1, -1), (0,), own_heads, out_weight, jnp.float32, WIDE
+            "project_sent_own_spatial",
+            (1, -1), (0,), (0,), [spatial_out], out_weight, jnp.float32, WIDE, sent,
         )
         low, high = project(
-            "project_sent", (1, -1), (1,), far_heads, out_weight, jnp.bfloat16, NARROW, sent
+            "project_sent",
+            (1, -1), (1,), (0,), [spatial_far], out_weight, jnp.bfloat16, NARROW, sent, True,
         )
         low = along_z(low, 1)
         high = along_z(high, -1)
+        head_arrays = [spatial_out, temporal_out, spatial_far, temporal_far]
         kept = project(
-            "project_kept", (0,), (0, 1), own_heads + far_heads, out_weight, jnp.bfloat16, NARROW
+            "project_kept", (0,), (0, 1), (0, 1), head_arrays, out_weight, jnp.bfloat16, NARROW
         )
         return combine(kept, low, high, gate_mod)[None]
 

time: 178 us -> 181 us (1.017)
  Pallas kernels: 73.2 us -> 76.8 us
    pallas_call x3 -> x4, Pallas kernels: 15.9 us -> 19.7 us  [project(): pl.pallas_call(lambda *refs: project_kernel(targets, groups, used, partia...]
  transfers between devices with their start and end apart: 14 -> 14, of which waited for: 8 -> 7; matrix products, arithmetic and copies ran while one was open for 2% -> 2% of each run, Pallas kernels for 35% -> 37%
where the time goes in v2:
time: 181 us
  Pallas kernels  76.8 us (42%)
  waiting for transfers between devices  34.6 us (19%)
  starting transfers between devices  30.3 us (17%)
  blocking collectives  16.1 us (9%)
  between operations  14.3 us (8%)
  local copies, waits for them, and re-layouts  6.45 us (4%)
  other arithmetic  2.02 us (1%)
    ppermute x11, waiting for transfers between devices, along_z(): lax.ppermute(value, 'frm', [(i, (i + shift) % planes) for i in range(plan...  27.2 us
    pallas_call x2, Pallas kernels, heads_both(): pl.pallas_call(lambda *refs: heads_both_kernel(parts, 2 * (buffers is not...  24.9 us
    ppermute x11, starting transfers between devices, along_z(): lax.ppermute(value, 'frm', [(i, (i + shift) % planes) for i in range(plan...  23.1 us
    pallas_call x4, Pallas kernels, project(): pl.pallas_call(lambda *refs: project_kernel(targets, groups, used, partia...  19.7 us
    all_to_all x1, blocking collectives, local(): spatial_out = lax.all_to_all(spatial_out, ('y', 'x'), 0, 0, tiled=True)  16.1 us
    pallas_call x2, Pallas kernels, spatial_attention(): pl.pallas_call(lambda *refs: spatial_kernel(side, *refs), in_specs=[whole...  13.8 us
    pallas_call x2, Pallas kernels, heads(): pl.pallas_call(body, grid=(pairs,), in_specs=in_specs, out_specs=pl.Block...  13.4 us
    all_to_all x1, waiting for transfers between devices, local(): lax.all_to_all(spatial.reshape(chips, tokens, 3 * HD), ('y', 'x'), 0, 0,...  7.37 us
  transfers between devices with their start and end apart: 14, of which 7 were waited for; matrix products, arithmetic and copies ran while one was open for 2% of the time, Pallas kernels for 37%

profile of v2, /device:TPU:0, one launch (start us, length us, event | category | flops | bytes accessed | tf_op | source)
XLA Modules:
  0.0 180.6 jit_solution(3605939503341875752)
XLA Ops:
  6.5 4.0 %collective-permute-start = (bf16[3,2,160,128]{3,2,1,0:T(8,128)(2,1)}, bf16[3,2,160,128]{3,2,1,0:T(8,128)(2,1)S(1)}, u32[]{:S(2)}, u32[]{:S(2)}) collective-permute-start(bf16[3,2,160,128]{3,2,1,0:T(8,128)(2,1)} %bitcast.50), channel_id=1, source_target_pairs={{0,2},{1,3},{2,0},{3,1},{4,6},{5,7},{6,4},{7,5},{8,10},{9,11},{10,... | collective-permute-start | bytes 737288 | tf_op jit(solution)/shard_map/gather_w_out/ppermute | solution.py:430
  10.6 1.3 copy-done.2
  11.9 0.7 copy-done.4
  12.6 0.7 copy-done.5
  13.4 1.8 %modulate.1 = (bf16[64,5120]{1,0:T(8,128)(2,1)}, bf16[64,5120]{1,0:T(8,128)(2,1)S(1)}) custom-call(bf16[128,5120]{1,0:T(8,128)(2,1)S(1)} %bitcast.41, f32[1,5120]{1,0:T(1,128)S(1)} %bitcast.44, f32[1,5120]{1,0:T(1,128)S(1)} %bitcast.45), custom_call_target="tpu_custom_call" | custom-call | flops 6553600 | bytes 2621440 | tf_op jit(solution)/shard_map/modulate/modulate/pallas_call | solution.py:46
  15.2 1.6 collective-permute-done
  16.8 1.8 pad_maximum_fusion
  18.5 1.4 collective-permute-start.1
  19.9 2.2 %collective-permute-start.2 = (bf16[64,5120]{1,0:T(8,128)(2,1)S(1)}, bf16[64,5120]{1,0:T(8,128)(2,1)}, u32[]{:S(2)}, u32[]{:S(2)}) collective-permute-start(bf16[64,5120]{1,0:T(8,128)(2,1)S(1)} %get-tuple-element.35.refs_1_), channel_id=1, source_target_pairs={{0,3},{1,0},{2,1},{3,2},{4,7},{5,4},{6,5},{7,6},{8,11},{9,8},{10,9... | collective-permute-start | bytes 1966088 | tf_op jit(solution)/shard_map/qkv/ppermute | solution.py:430
  22.1 1.9 %collective-permute-start.5 = (bf16[64,5120]{1,0:T(8,128)(2,1)}, bf16[64,5120]{1,0:T(8,128)(2,1)}, u32[]{:S(2)}, u32[]{:S(2)}) collective-permute-start(bf16[64,5120]{1,0:T(8,128)(2,1)} %get-tuple-element.34.refs_0_), channel_id=1, source_target_pairs={{0,3},{1,0},{2,1},{3,2},{4,7},{5,4},{6,5},{7,6},{8,11},{9,8},{10,9... | collective-permute-start | bytes 1966088 | tf_op jit(solution)/shard_map/qkv/ppermute | solution.py:430
  24.0 0.1 collective-permute-start.6
  24.2 10.5 %qkv_both.2 = (bf16[4,4,128,384]{3,2,1,0:T(8,128)(2,1)}, bf16[4,3,128,384]{3,2,1,0:T(8,128)(2,1)S(1)}) custom-call(bf16[64,5120]{1,0:T(8,128)(2,1)} %get-tuple-element.34.refs_0_, bf16[64,5120]{1,0:T(8,128)(2,1)S(1)} %get-tuple-element.35.refs_1_, bf16[3,6,5120,128]{3,2,1,0:T(8,128)(2,1)} %bitcast.46, f32[2,3,2,128]{3,2,1,0:T(2,128)S(1)} %fusion.refs_3_.refs_5_), custom_call_target="tpu_custom_call" | custom-call | flops 3019898880 | bytes 23592960 | tf_op jit(solution)/shard_map/qkv/qkv_both/pallas_call | solution.py:132
  34.7 3.2 %collective-permute-done.1.refs_2_ = bf16[64,5120]{1,0:T(8,128)(2,1)} collective-permute-done((bf16[64,5120]{1,0:T(8,128)(2,1)}, bf16[64,5120]{1,0:T(8,128)(2,1)}, u32[]{:S(2)}, u32[]{:S(2)}) %collective-permute-start.1) | collective-permute-done | bytes 655392 | tf_op jit(solution)/shard_map/qkv/ppermute | solution.py:430
  38.0 1.6 collective-permute-start.3
  39.6 1.6 collective-permute-start.4
  41.2 10.5 %collective-permute-done.5.refs_0_ = bf16[64,5120]{1,0:T(8,128)(2,1)} collective-permute-done((bf16[64,5120]{1,0:T(8,128)(2,1)}, bf16[64,5120]{1,0:T(8,128)(2,1)}, u32[]{:S(2)}, u32[]{:S(2)}) %collective-permute-start.5) | collective-permute-done | bytes 655392 | tf_op jit(solution)/shard_map/qkv/ppermute | solution.py:430
  51.7 0.3 collective-permute-done.6.refs_3_
  52.0 14.3 %qkv_both.3 = (bf16[4,4,128,384]{3,2,1,0:T(8,128)(2,1)}, bf16[4,3,128,384]{3,2,1,0:T(8,128)(2,1)S(1)}) custom-call(bf16[64,5120]{1,0:T(8,128)(2,1)} %collective-permute-done.5.refs_0_, bf16[64,5120]{1,0:T(8,128)(2,1)} %collective-permute-done.2.refs_1_, ...), custom_call_target="tpu_custom_call", output_to_operand_aliasing={{0}: (6, {}), {1}: (7, {})} | custom-call | flops 6039797760 | bytes 23592960 | tf_op jit(solution)/shard_map/qkv/qkv_both/pallas_call | solution.py:132
  66.3 7.2 %qkv_spatial.1 = bf16[4,4,128,384]{3,2,1,0:T(8,128)(2,1)} custom-call(bf16[64,5120]{1,0:T(8,128)(2,1)S(1)} %collective-permute-done.3.refs_0_, bf16[64,5120]{1,0:T(8,128)(2,1)S(1)} %collective-permute-done.4.refs_1_, bf16[3,6,5120,128]{3,2,1,0:T(8,128)(2,1)} %bitcast.48, f32[3,2,128]{2,1,0:T(2,128)S(1)} %get-tuple-element.62.refs_3_, ...), custom_call_target="tpu_custom_call", output_to_operand_aliasing={{}: (4, {})} | custom-call | flops 1509949440 | bytes 11796480 | tf_op jit(solution)/shard_map/qkv/qkv_spatial/pallas_call | solution.py:172
  73.5 7.2 %all-to-all-start = ((bf16[16,128,384]{2,1,0:T(8,128)(2,1)}), bf16[16,128,384]{2,1,0:T(8,128)(2,1)}, u32[]{:S(2)}, u32[]{:S(2)}) async-start(bf16[16,128,384]{2,1,0:T(8,128)(2,1)} %bitcast.8), calls=%async_computation | async-start | bytes 3145728 | tf_op jit(solution)/shard_map/spatial/all_to_all | solution.py:495
  80.8 0.6 dynamic_slice.23
  82.1 0.2 copy.30
  82.3 0.6 gather_fusion
  82.8 0.1 copy.26
  83.0 0.6 gather_fusion.1
  83.5 0.6 gather_fusion.2
  84.3 0.1 copy.27
  84.5 6.3 %qkv_temporal.1.qkv_ref = bf16[4,3,128,384]{3,2,1,0:T(8,128)(2,1)S(1)} custom-call(bf16[64,5120]{1,0:T(8,128)(2,1)S(1)} %collective-permute-done.3.refs_0_, bf16[64,5120]{1,0:T(8,128)(2,1)S(1)} %collective-permute-done.4.refs_1_, bf16[3,6,5120,128]{3,2,1,0:T(8,128)(2,1)} %bitcast.49, ...), custom_call_target="tpu_custom_call", output_to_operand_aliasing={{}: (4, {})} | custom-call | flops 1509949440 | bytes 11796480 | tf_op jit(solution)/shard_map/qkv/qkv_temporal/pallas_call | solution.py:172
  90.8 1.9 %temporal_attention.1.refs_1_.refs_0_ = bf16[4,3,128,128]{3,2,1,0:T(8,128)(2,1)S(1)} custom-call(bf16[4,3,128,384]{3,2,1,0:T(8,128)(2,1)S(1)} %qkv_temporal.1.qkv_ref, f32[3,4,1,512]{3,2,1,0:T(1,128)S(1)} %bitcast.42), custom_call_target="tpu_custom_call" | custom-call | flops 603979776 | bytes 1179648 | tf_op jit(solution)/shard_map/temporal/temporal_attention/pallas_call | solution.py:261
  92.7 3.5 %collective-permute-start.7 = (bf16[3,3,128,128]{3,2,1,0:T(8,128)(2,1)S(1)}, bf16[3,3,128,128]{3,2,1,0:T(8,128)(2,1)S(1)}, u32[]{:S(2)}, u32[]{:S(2)}) collective-permute-start(bf16[3,3,128,128]{3,2,1,0:T(8,128)(2,1)S(1)} %slice.24), channel_id=1, source_target_pairs={{0,2},{1,3},{2,0},{3,1},{4,6},{5,7},{6,4},{7,5},{8,10},{9,11},{10,... | collective-permute-start | bytes 884744 | tf_op jit(solution)/shard_map/temporal/ppermute | solution.py:430
  96.2 0.2 reshape.65
  96.3 0.1 constant_dynamic-slice_fusion.1
  96.5 0.2 copy.29
  96.7 0.2 copy.28
  96.9 4.1 %collective-permute-done.7.refs_3_.refs_1_ = bf16[3,3,128,128]{3,2,1,0:T(8,128)(2,1)S(1)} collective-permute-done((bf16[3,3,128,128]{3,2,1,0:T(8,128)(2,1)S(1)}, bf16[3,3,128,128]{3,2,1,0:T(8,128)(2,1)S(1)}, u32[]{:S(2)}, u32[]{:S(2)}) %collective-permute-start.7) | collective-permute-done | bytes 294944 | tf_op jit(solution)/shard_map/temporal/ppermute | solution.py:430
  101.0 7.4 %all-to-all-done.refs_0_.refs_1_ = bf16[16,128,384]{2,1,0:T(8,128)(2,1)} async-done(((bf16[16,128,384]{2,1,0:T(8,128)(2,1)}), bf16[16,128,384]{2,1,0:T(8,128)(2,1)}, u32[]{:S(2)}, u32[]{:S(2)}) %all-to-all-start) | async-done | bytes 1572896 | tf_op jit(solution)/shard_map/spatial/all_to_all | solution.py:495
  108.4 7.7 %spatial_attention_own.1.refs_3_ = f32[2048,256]{1,0:T(8,128)S(1)} custom-call(bf16[16,128,384]{2,1,0:T(8,128)(2,1)} %all-to-all-done.refs_0_.refs_1_, bf16[16,128,384]{2,1,0:T(8,128)(2,1)} %all-to-all-done.refs_0_.refs_1_, f32[32,128]{1,0:T(8,128)S(1)} %pad.4.refs_2_), custom_call_target="tpu_custom_call" | custom-call | flops 4294967296 | bytes 3145728 | tf_op jit(solution)/shard_map/spatial/spatial_attention_own/pallas_call | solution.py:230
  116.1 6.1 %spatial_attention_other.1 = bf16[16,128,128]{2,1,0:T(8,128)(2,1)S(1)} custom-call(bf16[16,128,384]{2,1,0:T(8,128)(2,1)} %all-to-all-done.refs_0_.refs_1_, bf16[16,128,384]{2,1,0:T(8,128)(2,1)S(1)} %collective-permute-done.8.refs_1_, f32[32,128]{1,0:T(8,128)S(1)} %pad.4.refs_2_, f32[2048,256]{1,0:T(8,128)S(1)} %spatial_attention_own.1.refs_3_), custom_call_target="tpu_custom_call" | custom-call | flops 4294967296 | bytes 3145728 | tf_op jit(solution)/shard_map/spatial/spatial_attention_other/pallas_call | solution.py:230
  122.2 16.1 %all_to_all.10 = bf16[16,128,128]{2,1,0:T(8,128)(2,1)S(1)} all-to-all(bf16[16,128,128]{2,1,0:T(8,128)(2,1)S(1)} %spatial_attention_other.1), channel_id=1, replica_groups=mesh['y'=4,'x'=4,'core'=2,'frm'=4] {'y','x'}, dimensions={0} | all-to-all | bytes 1048576 | tf_op jit(solution)/shard_map/spatial/all_to_all | solution.py:508
  138.4 3.5 %collective-permute-start.9 = (bf16[3,3,128,128]{3,2,1,0:T(8,128)(2,1)S(1)}, bf16[3,3,128,128]{3,2,1,0:T(8,128)(2,1)S(1)}, u32[]{:S(2)}, u32[]{:S(2)}) collective-permute-start(bf16[3,3,128,128]{3,2,1,0:T(8,128)(2,1)S(1)} %slice.25), channel_id=1, source_target_pairs={{0,2},{1,3},{2,0},{3,1},{4,6},{5,7},{6,4},{7,5},{8,10},{9,11},{10,... | collective-permute-start | bytes 884744 | tf_op jit(solution)/shard_map/spatial/ppermute | solution.py:430
  141.8 6.6 %project_sent_temporal.1.refs_2_ = f32[128,5120]{1,0:T(8,128)S(1)} custom-call(bf16[4,3,128,128]{3,2,1,0:T(8,128)(2,1)S(1)} %temporal_attention.1.refs_1_.refs_0_, bf16[3,3,128,128]{3,2,1,0:T(8,128)(2,1)S(1)} %collective-permute-done.7.refs_3_.refs_1_, bf16[32,2,3,2,160,128]{5,4,3,2,1,0:T(8,128)(2,1)} %bitcast.32), custom_call_target="tpu_custom_call" | custom-call | flops 1006632960 | bytes 7864320 | tf_op jit(solution)/shard_map/spatial/project_sent_temporal/pallas_call | solution.py:351
  148.5 4.8 %project_sent_own_spatial.1.refs_2_ = f32[128,5120]{1,0:T(8,128)S(1)} custom-call(bf16[4,4,128,128]{3,2,1,0:T(8,128)(2,1)S(1)} %bitcast.39, bf16[32,2,3,2,160,128]{5,4,3,2,1,0:T(8,128)(2,1)} %bitcast.33, f32[128,5120]{1,0:T(8,128)S(1)} %project_sent_temporal.1.refs_2_), custom_call_target="tpu_custom_call" | custom-call | flops 503316480 | bytes 3932160 | tf_op jit(solution)/shard_map/project/project_sent_own_spatial/pallas_call | solution.py:351
  153.3 2.5 %project_sent.1 = (bf16[128,2560]{1,0:T(8,128)(2,1)S(1)}, bf16[128,2560]{1,0:T(8,128)(2,1)S(1)}) custom-call(bf16[3,3,128,128]{3,2,1,0:T(8,128)(2,1)S(1)} %collective-permute-done.9.refs_2_.refs_0_, bf16[32,2,3,2,160,128]{5,4,3,2,1,0:T(8,128)(2,1)S(1)} %bitcast.36, f32[128,5120]{1,0:T(8,128)S(1)} %project_sent_own_spatial.1.refs_2_), custom_call_target="tpu_custom_call" | custom-call | flops 503316480 | bytes 3932160 | tf_op jit(solution)/shard_map/project/project_sent/pallas_call | solution.py:351
  155.9 0.7 collective-permute-start.10
  156.6 2.6 %collective-permute-start.11 = (bf16[128,2560]{1,0:T(8,128)(2,1)S(1)}, bf16[128,2560]{1,0:T(8,128)(2,1)S(1)}, u32[]{:S(2)}, u32[]{:S(2)}) collective-permute-start(bf16[128,2560]{1,0:T(8,128)(2,1)S(1)} %get-tuple-element.58), channel_id=1, source_target_pairs={{0,3},{1,0},{2,1},{3,2},{4,7},{5,4},{6,5},{7,6},{8,11},{9,8},{10,9... | collective-permute-start | bytes 1966088 | tf_op jit(solution)/shard_map/project/ppermute | solution.py:430
  159.2 5.7 %project_kept.1.own_ref = bf16[128,5120]{1,0:T(8,128)(2,1)S(1)} custom-call(bf16[4,4,128,128]{3,2,1,0:T(8,128)(2,1)S(1)} %bitcast.40, bf16[4,3,128,128]{3,2,1,0:T(8,128)(2,1)S(1)} %temporal_attention.1.refs_1_.refs_0_, bf16[3,3,128,128]{3,2,1,0:T(8,128)(2,1)S(1)} %collective-permute-done.9.refs_2_.refs_0_, ...), custom_call_target="tpu_custom_call" | custom-call | flops 2013265920 | bytes 15728640 | tf_op jit(solution)/shard_map/project/project_kept/pallas_call | solution.py:351
  164.9 7.4 %collective-permute-done.10.low_ref = bf16[128,2560]{1,0:T(8,128)(2,1)S(1)} collective-permute-done((bf16[128,2560]{1,0:T(8,128)(2,1)S(1)}, bf16[128,2560]{1,0:T(8,128)(2,1)S(1)}, u32[]{:S(2)}, u32[]{:S(2)}) %collective-permute-start.10) | collective-permute-done | bytes 655392 | tf_op jit(solution)/shard_map/project/ppermute | solution.py:430
  172.3 1.4 combine.1
  (53 shorter events, 0.6 us)
Async XLA Ops:
  6.5 89.6 %copy-start = (s32[3,4,32,32]{3,2,1,0:T(8,128)S(1)}, s32[3,4,32,32]{3,2,1,0:T(8,128)}, u32[]{:S(2)}) copy-start(s32[3,4,32,32]{3,2,1,0:T(8,128)} %param.20) | copy-start | bytes 147460
  6.5 17.6 %copy-start.8 = (f32[2]{0:T(128)S(1)}, f32[2]{0:T(128)}, u32[]{:S(2)}) copy-start(f32[2]{0:T(128)} %constant.151.clone) | copy-start | bytes 28
  6.5 17.6 %copy-start.7 = (f32[3,4,128]{2,1,0:T(4,128)S(1)}, f32[3,4,128]{2,1,0:T(4,128)}, u32[]{:S(2)}) copy-start(f32[3,4,128]{2,1,0:T(4,128)} %param.18) | copy-start | bytes 18436
  6.5 101.8 %all-gather.3.cloned.1.call-start = ((), (), s32[]{:S(2)}) async-start(), calls=%async_computation.2 | async-start | bytes 16220160 | tf_op jit(solution)/shard_map/gather_w_out/all_gather | solution.py:442
  6.5 10.2 %collective-permute-start = (bf16[3,2,160,128]{3,2,1,0:T(8,128)(2,1)}, bf16[3,2,160,128]{3,2,1,0:T(8,128)(2,1)S(1)}, u32[]{:S(2)}, u32[]{:S(2)}) collective-permute-start(bf16[3,2,160,128]{3,2,1,0:T(8,128)(2,1)} %bitcast.50), channel_id=1, source_target_pairs={{0,2},{1,3},{2,0},{3,1},{4,6},{5,7},{6,4},{7,5},{8,10},{9,11},{10,... | collective-permute-start | bytes 737288 | tf_op jit(solution)/shard_map/gather_w_out/ppermute | solution.py:430
  10.6 1.3 copy-start.2
  11.9 0.7 copy-start.4
  12.6 0.7 copy-start.5
  18.5 19.4 %collective-permute-start.1 = (bf16[64,5120]{1,0:T(8,128)(2,1)}, bf16[64,5120]{1,0:T(8,128)(2,1)}, u32[]{:S(2)}, u32[]{:S(2)}) collective-permute-start(bf16[64,5120]{1,0:T(8,128)(2,1)} %get-tuple-element.34.refs_0_), channel_id=1, source_target_pairs={{0,1},{1,2},{2,3},{3,0},{4,5},{5,6},{6,7},{7,4},{8,9},{9,10},{10,1... | collective-permute-start | bytes 1966088 | tf_op jit(solution)/shard_map/qkv/ppermute | solution.py:430
  19.9 18.1 %collective-permute-start.2 = (bf16[64,5120]{1,0:T(8,128)(2,1)S(1)}, bf16[64,5120]{1,0:T(8,128)(2,1)}, u32[]{:S(2)}, u32[]{:S(2)}) collective-permute-start(bf16[64,5120]{1,0:T(8,128)(2,1)S(1)} %get-tuple-element.35.refs_1_), channel_id=1, source_target_pairs={{0,3},{1,0},{2,1},{3,2},{4,7},{5,4},{6,5},{7,6},{8,11},{9,8},{10,9... | collective-permute-start | bytes 1966088 | tf_op jit(solution)/shard_map/qkv/ppermute | solution.py:430
  22.1 29.6 %collective-permute-start.5 = (bf16[64,5120]{1,0:T(8,128)(2,1)}, bf16[64,5120]{1,0:T(8,128)(2,1)}, u32[]{:S(2)}, u32[]{:S(2)}) collective-permute-start(bf16[64,5120]{1,0:T(8,128)(2,1)} %get-tuple-element.34.refs_0_), channel_id=1, source_target_pairs={{0,3},{1,0},{2,1},{3,2},{4,7},{5,4},{6,5},{7,6},{8,11},{9,8},{10,9... | collective-permute-start | bytes 1966088 | tf_op jit(solution)/shard_map/qkv/ppermute | solution.py:430
  24.0 28.0 %collective-permute-start.6 = (bf16[64,5120]{1,0:T(8,128)(2,1)S(1)}, bf16[64,5120]{1,0:T(8,128)(2,1)}, u32[]{:S(2)}, u32[]{:S(2)}) collective-permute-start(bf16[64,5120]{1,0:T(8,128)(2,1)S(1)} %get-tuple-element.35.refs_1_), channel_id=1, source_target_pairs={{0,1},{1,2},{2,3},{3,0},{4,5},{5,6},{6,7},{7,4},{8,9},{9,10},{10,1... | collective-permute-start | bytes 1966088 | tf_op jit(solution)/shard_map/qkv/ppermute | solution.py:430
  38.0 28.4 %collective-permute-start.3 = (bf16[64,5120]{1,0:T(8,128)(2,1)}, bf16[64,5120]{1,0:T(8,128)(2,1)S(1)}, u32[]{:S(2)}, u32[]{:S(2)}) collective-permute-start(bf16[64,5120]{1,0:T(8,128)(2,1)} %collective-permute-done.1.refs_2_), channel_id=1, source_target_pairs={{0,1},{1,2},{2,3},{3,0},{4,5},{5,6},{6,7},{7,4},{8,9},{9,10},{10,1... | collective-permute-start | bytes 1966088 | tf_op jit(solution)/shard_map/qkv/ppermute | solution.py:430
  39.6 26.8 %collective-permute-start.4 = (bf16[64,5120]{1,0:T(8,128)(2,1)}, bf16[64,5120]{1,0:T(8,128)(2,1)S(1)}, u32[]{:S(2)}, u32[]{:S(2)}) collective-permute-start(bf16[64,5120]{1,0:T(8,128)(2,1)} %collective-permute-done.2.refs_1_), channel_id=1, source_target_pairs={{0,3},{1,0},{2,1},{3,2},{4,7},{5,4},{6,5},{7,6},{8,11},{9,8},{10,9... | collective-permute-start | bytes 1966088 | tf_op jit(solution)/shard_map/qkv/ppermute | solution.py:430
  73.5 7.2 %copy-start.6 = (s32[3,32,4,4]{1,3,2,0:T(4,128)S(1)}, s32[3,32,4,4]{1,3,2,0:T(4,128)}, u32[]{:S(2)}) copy-start(s32[3,32,4,4]{1,3,2,0:T(4,128)} %param.21) | copy-start | bytes 18436
  73.5 7.3 %copy-start.10 = (s32[4]{0:T(128)S(1)}, s32[4]{0:T(128)}, u32[]{:S(2)}) copy-start(s32[4]{0:T(128)} %constant.152.clone) | copy-start | bytes 52
  73.5 10.0 %copy-start.9 = (s32[4]{0:T(128)S(1)}, s32[4]{0:T(128)}, u32[]{:S(2)}) copy-start(s32[4]{0:T(128)} %param.22) | copy-start | bytes 52
  73.5 34.9 %all-to-all-start = ((bf16[16,128,384]{2,1,0:T(8,128)(2,1)}), bf16[16,128,384]{2,1,0:T(8,128)(2,1)}, u32[]{:S(2)}, u32[]{:S(2)}) async-start(bf16[16,128,384]{2,1,0:T(8,128)(2,1)} %bitcast.8), calls=%async_computation | async-start | bytes 3145728 | tf_op jit(solution)/shard_map/spatial/all_to_all | solution.py:495
  92.7 8.3 %collective-permute-start.7 = (bf16[3,3,128,128]{3,2,1,0:T(8,128)(2,1)S(1)}, bf16[3,3,128,128]{3,2,1,0:T(8,128)(2,1)S(1)}, u32[]{:S(2)}, u32[]{:S(2)}) collective-permute-start(bf16[3,3,128,128]{3,2,1,0:T(8,128)(2,1)S(1)} %slice.24), channel_id=1, source_target_pairs={{0,2},{1,3},{2,0},{3,1},{4,6},{5,7},{6,4},{7,5},{8,10},{9,11},{10,... | collective-permute-start | bytes 884744 | tf_op jit(solution)/shard_map/temporal/ppermute | solution.py:430
  108.4 7.7 %collective-permute-start.8 = (bf16[16,128,384]{2,1,0:T(8,128)(2,1)}, bf16[16,128,384]{2,1,0:T(8,128)(2,1)S(1)}, u32[]{:S(2)}, u32[]{:S(2)}) collective-permute-start(bf16[16,128,384]{2,1,0:T(8,128)(2,1)} %all-to-all-done.refs_0_.refs_1_), channel_id=1, source_target_pairs={{0,4},{4,0},{1,5},{5,1},{2,6},{6,2},{3,7},{7,3},{8,12},{12,8},{9,1... | collective-permute-start | bytes 4718600 | tf_op jit(solution)/shard_map/spatial/ppermute | solution.py:433
  138.4 14.9 %collective-permute-start.9 = (bf16[3,3,128,128]{3,2,1,0:T(8,128)(2,1)S(1)}, bf16[3,3,128,128]{3,2,1,0:T(8,128)(2,1)S(1)}, u32[]{:S(2)}, u32[]{:S(2)}) collective-permute-start(bf16[3,3,128,128]{3,2,1,0:T(8,128)(2,1)S(1)} %slice.25), channel_id=1, source_target_pairs={{0,2},{1,3},{2,0},{3,1},{4,6},{5,7},{6,4},{7,5},{8,10},{9,11},{10,... | collective-permute-start | bytes 884744 | tf_op jit(solution)/shard_map/spatial/ppermute | solution.py:430
  141.8 11.4 %slice-start = ((s8[15728640]{0:T(1024)(128)(4,1)}), s8[4194304]{0:T(1024)(128)(4,1)S(1)}, s32[]{:S(2)}) async-start(s8[15728640]{0:T(1024)(128)(4,1)} %bitcast.34), calls=%async_computation.3 | async-start | bytes 8388608
  141.8 11.4 %slice-start.1 = ((s8[15728640]{0:T(1024)(128)(4,1)}), s8[4194304]{0:T(1024)(128)(4,1)S(1)}, s32[]{:S(2)}) async-start(s8[15728640]{0:T(1024)(128)(4,1)} %bitcast.34), calls=%async_computation.4 | async-start | bytes 8388608
  148.4 4.8 %slice-start.2 = ((s8[15728640]{0:T(1024)(128)(4,1)}), s8[4194304]{0:T(1024)(128)(4,1)S(1)}, s32[]{:S(2)}) async-start(s8[15728640]{0:T(1024)(128)(4,1)} %bitcast.34), calls=%async_computation.5 | async-start | bytes 8388608
  148.4 4.8 %slice-start.3 = ((s8[15728640]{0:T(1024)(128)(4,1)}), s8[3145728]{0:T(1024)(128)(4,1)S(1)}, s32[]{:S(2)}) async-start(s8[15728640]{0:T(1024)(128)(4,1)} %bitcast.34), calls=%async_computation.6 | async-start | bytes 6291456
  155.9 16.5 %collective-permute-start.10 = (bf16[128,2560]{1,0:T(8,128)(2,1)S(1)}, bf16[128,2560]{1,0:T(8,128)(2,1)S(1)}, u32[]{:S(2)}, u32[]{:S(2)}) collective-permute-start(bf16[128,2560]{1,0:T(8,128)(2,1)S(1)} %get-tuple-element.57), channel_id=1, source_target_pairs={{0,1},{1,2},{2,3},{3,0},{4,5},{5,6},{6,7},{7,4},{8,9},{9,10},{10,1... | collective-permute-start | bytes 1966088 | tf_op jit(solution)/shard_map/project/ppermute | solution.py:430
  156.6 15.7 %copy-start.3 = (f32[5120]{0:T(1024)S(1)}, f32[5120]{0:T(1024)}, u32[]{:S(2)}) copy-start(f32[5120]{0:T(1024)} %param.16) | copy-start | bytes 61444
  156.6 15.7 %collective-permute-start.11 = (bf16[128,2560]{1,0:T(8,128)(2,1)S(1)}, bf16[128,2560]{1,0:T(8,128)(2,1)S(1)}, u32[]{:S(2)}, u32[]{:S(2)}) collective-permute-start(bf16[128,2560]{1,0:T(8,128)(2,1)S(1)} %get-tuple-element.58), channel_id=1, source_target_pairs={{0,3},{1,0},{2,1},{3,2},{4,7},{5,4},{6,5},{7,6},{8,11},{9,8},{10,9... | collective-permute-start | bytes 1966088 | tf_op jit(solution)/shard_map/project/ppermute | solution.py:430
  172.3 1.4 copy-start.1
Sparse Core Ops, SparseCore 0:
  18.7 87.2 all-gather.2

commit v3 on v1

--- a/solution.py
+++ b/solution.py
@@ -326,7 +326,7 @@
 
 def project(name, targets, groups, head_arrays, weight, dtype, limit, partial=None):
     shards, _, pairs, kinds, shard, _ = weight.shape
-    per_step = 8
+    per_step = 8 if partial is None else 16
     steps, width = shards // per_step, per_step * shard
     depth = len(groups) * kinds * pairs * HD
     first = groups[0] // len(groups)
@@ -504,7 +504,7 @@
             "project_sent_own_group", (1, -1), (0,), own_heads, out_weight, jnp.float32, WIDE
         )
         low, high = project(
-            "project_sent", (1, -1), (1,), far_heads, out_weight, jnp.bfloat16, NARROW, sent
+            "project_sent", (1, -1), (1,), far_heads, out_weight, jnp.bfloat16, 24 * 1024 * 1024, sent
         )
         low = along_z(low, 1)
         high = along_z(high, -1)

time: 178 us -> 177 us (level)
  no operation moved by 1% of the time
where the time goes in v3:
time: 177 us; the launch traced here: 176 us
  Pallas kernels  72.5 us (41%)
  waiting for transfers between devices  34.7 us (20%)
  starting transfers between devices  30.3 us (17%)
  blocking collectives  16.1 us (9%)
  between operations  14.3 us (8%)
  local copies, waits for them, and re-layouts  6.45 us (4%)
  other arithmetic  2.03 us (1%)
    ppermute x11, waiting for transfers between devices, along_z(): lax.ppermute(value, 'frm', [(i, (i + shift) % planes) for i in range(plan...  27.3 us
    pallas_call x2, Pallas kernels, heads_both(): pl.pallas_call(lambda *refs: heads_both_kernel(parts, 2 * (buffers is not...  24.8 us
    ppermute x11, starting transfers between devices, along_z(): lax.ppermute(value, 'frm', [(i, (i + shift) % planes) for i in range(plan...  23.1 us
    all_to_all x1, blocking collectives, local(): spatial_out = lax.all_to_all(spatial_out, ('y', 'x'), 0, 0, tiled=True)  16.1 us
    pallas_call x3, Pallas kernels, project(): pl.pallas_call(lambda *refs: project_kernel(targets, groups, *refs), grid...  15.2 us
    pallas_call x2, Pallas kernels, spatial_attention(): pl.pallas_call(lambda *refs: spatial_kernel(side, *refs), in_specs=[whole...  14 us
    pallas_call x2, Pallas kernels, heads(): pl.pallas_call(body, grid=(pairs,), in_specs=in_specs, out_specs=pl.Block...  13.4 us
    all_to_all x1, waiting for transfers between devices, local(): lax.all_to_all(spatial.reshape(chips, tokens, 3 * HD), ('y', 'x'), 0, 0,...  7.37 us
  transfers between devices with their start and end apart: 14, of which 8 were waited for; matrix products, arithmetic and copies ran while one was open for 2% of the time, Pallas kernels for 35%

profile of v3, /device:TPU:0, one launch (start us, length us, event | category | flops | bytes accessed | tf_op | source)
XLA Modules:
  0.0 176.3 jit_solution(13825404670720523624)
XLA Ops:
  6.5 4.0 %collective-permute-start = (bf16[3,2,160,128]{3,2,1,0:T(8,128)(2,1)}, bf16[3,2,160,128]{3,2,1,0:T(8,128)(2,1)S(1)}, u32[]{:S(2)}, u32[]{:S(2)}) collective-permute-start(bf16[3,2,160,128]{3,2,1,0:T(8,128)(2,1)} %bitcast.49), channel_id=1, source_target_pairs={{0,2},{1,3},{2,0},{3,1},{4,6},{5,7},{6,4},{7,5},{8,10},{9,11},{10,... | collective-permute-start | bytes 737288 | tf_op jit(solution)/shard_map/gather_w_out/ppermute | solution.py:423
  10.6 1.3 copy-done.1
  11.9 0.7 copy-done.3
  12.6 0.7 copy-done.4
  13.4 1.8 %modulate.1 = (bf16[64,5120]{1,0:T(8,128)(2,1)}, bf16[64,5120]{1,0:T(8,128)(2,1)S(1)}) custom-call(bf16[128,5120]{1,0:T(8,128)(2,1)S(1)} %bitcast.40, f32[1,5120]{1,0:T(1,128)S(1)} %bitcast.43, f32[1,5120]{1,0:T(1,128)S(1)} %bitcast.44), custom_call_target="tpu_custom_call" | custom-call | flops 6553600 | bytes 2621440 | tf_op jit(solution)/shard_map/modulate/modulate/pallas_call | solution.py:46
  15.2 1.6 collective-permute-done
  16.8 1.8 %pad_maximum_fusion = bf16[2,3,2,160,128]{4,3,2,1,0:T(8,128)(2,1)} fusion(bf16[1,3,2,160,128]{4,3,2,1,0:T(8,128)(2,1)S(1)} %bitcast.51, bf16[1,3,2,160,128]{4,3,2,1,0:T(8,128)(2,1)} %bitcast.50), kind=kLoop, calls=%fused_computation.3 | loop fusion | flops 245760 | bytes 983040 | tf_op jit(solution)/shard_map/gather_w_out/stack | solution.py:434
  18.5 1.4 collective-permute-start.1
  19.9 2.2 %collective-permute-start.2 = (bf16[64,5120]{1,0:T(8,128)(2,1)S(1)}, bf16[64,5120]{1,0:T(8,128)(2,1)}, u32[]{:S(2)}, u32[]{:S(2)}) collective-permute-start(bf16[64,5120]{1,0:T(8,128)(2,1)S(1)} %get-tuple-element.35.refs_1_), channel_id=1, source_target_pairs={{0,3},{1,0},{2,1},{3,2},{4,7},{5,4},{6,5},{7,6},{8,11},{9,8},{10,9... | collective-permute-start | bytes 1966088 | tf_op jit(solution)/shard_map/qkv/ppermute | solution.py:423
  22.1 1.9 %collective-permute-start.5 = (bf16[64,5120]{1,0:T(8,128)(2,1)}, bf16[64,5120]{1,0:T(8,128)(2,1)}, u32[]{:S(2)}, u32[]{:S(2)}) collective-permute-start(bf16[64,5120]{1,0:T(8,128)(2,1)} %get-tuple-element.34.refs_0_), channel_id=1, source_target_pairs={{0,3},{1,0},{2,1},{3,2},{4,7},{5,4},{6,5},{7,6},{8,11},{9,8},{10,9... | collective-permute-start | bytes 1966088 | tf_op jit(solution)/shard_map/qkv/ppermute | solution.py:423
  24.0 0.1 collective-permute-start.6
  24.2 10.5 %qkv_both.2 = (bf16[4,4,128,384]{3,2,1,0:T(8,128)(2,1)}, bf16[4,3,128,384]{3,2,1,0:T(8,128)(2,1)S(1)}) custom-call(bf16[64,5120]{1,0:T(8,128)(2,1)} %get-tuple-element.34.refs_0_, bf16[64,5120]{1,0:T(8,128)(2,1)S(1)} %get-tuple-element.35.refs_1_, bf16[3,6,5120,128]{3,2,1,0:T(8,128)(2,1)} %bitcast.45, f32[2,3,2,128]{3,2,1,0:T(2,128)S(1)} %fusion.refs_3_.refs_5_), custom_call_target="tpu_custom_call" | custom-call | flops 3019898880 | bytes 23592960 | tf_op jit(solution)/shard_map/qkv/qkv_both/pallas_call | solution.py:132
  34.7 3.2 %collective-permute-done.1.refs_2_ = bf16[64,5120]{1,0:T(8,128)(2,1)} collective-permute-done((bf16[64,5120]{1,0:T(8,128)(2,1)}, bf16[64,5120]{1,0:T(8,128)(2,1)}, u32[]{:S(2)}, u32[]{:S(2)}) %collective-permute-start.1) | collective-permute-done | bytes 655392 | tf_op jit(solution)/shard_map/qkv/ppermute | solution.py:423
  38.0 1.6 collective-permute-start.3
  39.6 1.6 collective-permute-start.4
  41.2 10.5 %collective-permute-done.5.refs_0_ = bf16[64,5120]{1,0:T(8,128)(2,1)} collective-permute-done((bf16[64,5120]{1,0:T(8,128)(2,1)}, bf16[64,5120]{1,0:T(8,128)(2,1)}, u32[]{:S(2)}, u32[]{:S(2)}) %collective-permute-start.5) | collective-permute-done | bytes 655392 | tf_op jit(solution)/shard_map/qkv/ppermute | solution.py:423
  51.7 0.3 collective-permute-done.6.refs_3_
  52.0 14.3 %qkv_both.3 = (bf16[4,4,128,384]{3,2,1,0:T(8,128)(2,1)}, bf16[4,3,128,384]{3,2,1,0:T(8,128)(2,1)S(1)}) custom-call(bf16[64,5120]{1,0:T(8,128)(2,1)} %collective-permute-done.5.refs_0_, bf16[64,5120]{1,0:T(8,128)(2,1)} %collective-permute-done.2.refs_1_, ...), custom_call_target="tpu_custom_call", output_to_operand_aliasing={{0}: (6, {}), {1}: (7, {})} | custom-call | flops 6039797760 | bytes 23592960 | tf_op jit(solution)/shard_map/qkv/qkv_both/pallas_call | solution.py:132
  66.3 7.2 %qkv_spatial.1 = bf16[4,4,128,384]{3,2,1,0:T(8,128)(2,1)} custom-call(bf16[64,5120]{1,0:T(8,128)(2,1)S(1)} %collective-permute-done.3.refs_0_, bf16[64,5120]{1,0:T(8,128)(2,1)S(1)} %collective-permute-done.4.refs_1_, bf16[3,6,5120,128]{3,2,1,0:T(8,128)(2,1)} %bitcast.47, f32[3,2,128]{2,1,0:T(2,128)S(1)} %get-tuple-element.62.refs_3_, ...), custom_call_target="tpu_custom_call", output_to_operand_aliasing={{}: (4, {})} | custom-call | flops 1509949440 | bytes 11796480 | tf_op jit(solution)/shard_map/qkv/qkv_spatial/pallas_call | solution.py:172
  73.5 7.2 %all-to-all-start = ((bf16[16,128,384]{2,1,0:T(8,128)(2,1)}), bf16[16,128,384]{2,1,0:T(8,128)(2,1)}, u32[]{:S(2)}, u32[]{:S(2)}) async-start(bf16[16,128,384]{2,1,0:T(8,128)(2,1)} %bitcast.8), calls=%async_computation | async-start | bytes 3145728 | tf_op jit(solution)/shard_map/spatial/all_to_all | solution.py:488
  80.8 0.6 dynamic_slice.23
  82.1 0.2 copy.30
  82.3 0.6 gather_fusion
  82.9 0.1 copy.26
  83.0 0.6 gather_fusion.1
  83.6 0.6 gather_fusion.2
  84.4 0.1 copy.27
  84.5 6.2 %qkv_temporal.1.qkv_ref = bf16[4,3,128,384]{3,2,1,0:T(8,128)(2,1)S(1)} custom-call(bf16[64,5120]{1,0:T(8,128)(2,1)S(1)} %collective-permute-done.3.refs_0_, bf16[64,5120]{1,0:T(8,128)(2,1)S(1)} %collective-permute-done.4.refs_1_, bf16[3,6,5120,128]{3,2,1,0:T(8,128)(2,1)} %bitcast.48, ...), custom_call_target="tpu_custom_call", output_to_operand_aliasing={{}: (4, {})} | custom-call | flops 1509949440 | bytes 11796480 | tf_op jit(solution)/shard_map/qkv/qkv_temporal/pallas_call | solution.py:172
  90.8 1.9 %temporal_attention.1.refs_1_ = bf16[4,3,128,128]{3,2,1,0:T(8,128)(2,1)S(1)} custom-call(bf16[4,3,128,384]{3,2,1,0:T(8,128)(2,1)S(1)} %qkv_temporal.1.qkv_ref, f32[3,4,1,512]{3,2,1,0:T(1,128)S(1)} %bitcast.41), custom_call_target="tpu_custom_call" | custom-call | flops 603979776 | bytes 1179648 | tf_op jit(solution)/shard_map/temporal/temporal_attention/pallas_call | solution.py:261
  92.7 3.5 %collective-permute-start.7 = (bf16[3,3,128,128]{3,2,1,0:T(8,128)(2,1)S(1)}, bf16[3,3,128,128]{3,2,1,0:T(8,128)(2,1)S(1)}, u32[]{:S(2)}, u32[]{:S(2)}) collective-permute-start(bf16[3,3,128,128]{3,2,1,0:T(8,128)(2,1)S(1)} %slice.24), channel_id=1, source_target_pairs={{0,2},{1,3},{2,0},{3,1},{4,6},{5,7},{6,4},{7,5},{8,10},{9,11},{10,... | collective-permute-start | bytes 884744 | tf_op jit(solution)/shard_map/temporal/ppermute | solution.py:423
  96.2 0.2 reshape.65
  96.3 0.1 constant_dynamic-slice_fusion.1
  96.5 0.2 copy.28
  96.7 0.2 copy.29
  96.9 4.1 %collective-permute-done.7.refs_3_.refs_1_ = bf16[3,3,128,128]{3,2,1,0:T(8,128)(2,1)S(1)} collective-permute-done((bf16[3,3,128,128]{3,2,1,0:T(8,128)(2,1)S(1)}, bf16[3,3,128,128]{3,2,1,0:T(8,128)(2,1)S(1)}, u32[]{:S(2)}, u32[]{:S(2)}) %collective-permute-start.7) | collective-permute-done | bytes 294944 | tf_op jit(solution)/shard_map/temporal/ppermute | solution.py:423
  101.0 7.4 %all-to-all-done.refs_0_.refs_1_ = bf16[16,128,384]{2,1,0:T(8,128)(2,1)} async-done(((bf16[16,128,384]{2,1,0:T(8,128)(2,1)}), bf16[16,128,384]{2,1,0:T(8,128)(2,1)}, u32[]{:S(2)}, u32[]{:S(2)}) %all-to-all-start) | async-done | bytes 1572896 | tf_op jit(solution)/shard_map/spatial/all_to_all | solution.py:488
  108.4 7.7 %spatial_attention_own.1.refs_3_ = f32[2048,256]{1,0:T(8,128)S(1)} custom-call(bf16[16,128,384]{2,1,0:T(8,128)(2,1)} %all-to-all-done.refs_0_.refs_1_, bf16[16,128,384]{2,1,0:T(8,128)(2,1)} %all-to-all-done.refs_0_.refs_1_, f32[32,128]{1,0:T(8,128)S(1)} %pad.4.refs_2_), custom_call_target="tpu_custom_call" | custom-call | flops 4294967296 | bytes 3145728 | tf_op jit(solution)/shard_map/spatial/spatial_attention_own/pallas_call | solution.py:230
  116.1 6.2 %spatial_attention_other.1 = bf16[16,128,128]{2,1,0:T(8,128)(2,1)S(1)} custom-call(bf16[16,128,384]{2,1,0:T(8,128)(2,1)} %all-to-all-done.refs_0_.refs_1_, bf16[16,128,384]{2,1,0:T(8,128)(2,1)S(1)} %collective-permute-done.8.refs_1_, f32[32,128]{1,0:T(8,128)S(1)} %pad.4.refs_2_, f32[2048,256]{1,0:T(8,128)S(1)} %spatial_attention_own.1.refs_3_), custom_call_target="tpu_custom_call" | custom-call | flops 4294967296 | bytes 3145728 | tf_op jit(solution)/shard_map/spatial/spatial_attention_other/pallas_call | solution.py:230
  122.4 16.1 %all_to_all.10 = bf16[16,128,128]{2,1,0:T(8,128)(2,1)S(1)} all-to-all(bf16[16,128,128]{2,1,0:T(8,128)(2,1)S(1)} %spatial_attention_other.1), channel_id=1, replica_groups=mesh['y'=4,'x'=4,'core'=2,'frm'=4] {'y','x'}, dimensions={0} | all-to-all | bytes 1048576 | tf_op jit(solution)/shard_map/spatial/all_to_all | solution.py:497
  138.6 3.4 %collective-permute-start.9 = (bf16[3,3,128,128]{3,2,1,0:T(8,128)(2,1)S(1)}, bf16[3,3,128,128]{3,2,1,0:T(8,128)(2,1)S(1)}, u32[]{:S(2)}, u32[]{:S(2)}) collective-permute-start(bf16[3,3,128,128]{3,2,1,0:T(8,128)(2,1)S(1)} %slice.25), channel_id=1, source_target_pairs={{0,2},{1,3},{2,0},{3,1},{4,6},{5,7},{6,4},{7,5},{8,10},{9,11},{10,... | collective-permute-start | bytes 884744 | tf_op jit(solution)/shard_map/spatial/ppermute | solution.py:423
  142.0 5.8 %project_sent_own_group.1.refs_3_ = f32[128,5120]{1,0:T(8,128)S(1)} custom-call(bf16[4,4,128,128]{3,2,1,0:T(8,128)(2,1)S(1)} %bitcast.38, bf16[4,3,128,128]{3,2,1,0:T(8,128)(2,1)S(1)} %temporal_attention.1.refs_1_, bf16[32,2,3,2,160,128]{5,4,3,2,1,0:T(8,128)(2,1)} %bitcast.32), custom_call_target="tpu_custom_call" | custom-call | flops 1006632960 | bytes 7864320 | tf_op jit(solution)/shard_map/project/project_sent_own_group/pallas_call | solution.py:344
  147.9 0.3 collective-permute-done.9.refs_2_.refs_0_
  148.2 3.7 %project_sent.1 = (bf16[128,2560]{1,0:T(8,128)(2,1)S(1)}, bf16[128,2560]{1,0:T(8,128)(2,1)S(1)}) custom-call(bf16[3,3,128,128]{3,2,1,0:T(8,128)(2,1)S(1)} %collective-permute-done.9.refs_2_.refs_0_, bf16[3,3,128,128]{3,2,1,0:T(8,128)(2,1)S(1)} %collective-permute-done.7.refs_3_.refs_1_, bf16[32,2,3,2,160,128]{5,4,3,2,1,0:T(8,128)(2,1)S(1)} %bitcast.35, ...), custom_call_target="tpu_custom_call" | custom-call | flops 1006632960 | bytes 7864320 | tf_op jit(solution)/shard_map/project/project_sent/pallas_call | solution.py:344
  151.8 1.6 collective-permute-start.10
  153.5 1.7 collective-permute-start.11
  155.1 5.7 %project_kept.1.own_ref = bf16[128,5120]{1,0:T(8,128)(2,1)S(1)} custom-call(bf16[4,4,128,128]{3,2,1,0:T(8,128)(2,1)S(1)} %bitcast.39, bf16[4,3,128,128]{3,2,1,0:T(8,128)(2,1)S(1)} %temporal_attention.1.refs_1_, bf16[3,3,128,128]{3,2,1,0:T(8,128)(2,1)S(1)} %collective-permute-done.9.refs_2_.refs_0_, ...), custom_call_target="tpu_custom_call" | custom-call | flops 2013265920 | bytes 15728640 | tf_op jit(solution)/shard_map/project/project_kept/pallas_call | solution.py:344
  160.9 7.2 %collective-permute-done.10.low_ref = bf16[128,2560]{1,0:T(8,128)(2,1)S(1)} collective-permute-done((bf16[128,2560]{1,0:T(8,128)(2,1)S(1)}, bf16[128,2560]{1,0:T(8,128)(2,1)S(1)}, u32[]{:S(2)}, u32[]{:S(2)}) %collective-permute-start.10) | collective-permute-done | bytes 655392 | tf_op jit(solution)/shard_map/project/ppermute | solution.py:423
  168.1 1.4 combine.1
  (50 shorter events, 0.6 us)
Async XLA Ops:
  6.5 89.6 %copy-start = (s32[3,4,32,32]{3,2,1,0:T(8,128)S(1)}, s32[3,4,32,32]{3,2,1,0:T(8,128)}, u32[]{:S(2)}) copy-start(s32[3,4,32,32]{3,2,1,0:T(8,128)} %param.20) | copy-start | bytes 147460
  6.5 17.6 %copy-start.7 = (f32[2]{0:T(128)S(1)}, f32[2]{0:T(128)}, u32[]{:S(2)}) copy-start(f32[2]{0:T(128)} %constant.151.clone) | copy-start | bytes 28
  6.5 17.6 %copy-start.6 = (f32[3,4,128]{2,1,0:T(4,128)S(1)}, f32[3,4,128]{2,1,0:T(4,128)}, u32[]{:S(2)}) copy-start(f32[3,4,128]{2,1,0:T(4,128)} %param.18) | copy-start | bytes 18436
  6.5 101.8 %all-gather.3.cloned.1.call-start = ((), (), s32[]{:S(2)}) async-start(), calls=%async_computation.2 | async-start | bytes 16220160 | tf_op jit(solution)/shard_map/gather_w_out/all_gather | solution.py:435
  6.5 10.2 %collective-permute-start = (bf16[3,2,160,128]{3,2,1,0:T(8,128)(2,1)}, bf16[3,2,160,128]{3,2,1,0:T(8,128)(2,1)S(1)}, u32[]{:S(2)}, u32[]{:S(2)}) collective-permute-start(bf16[3,2,160,128]{3,2,1,0:T(8,128)(2,1)} %bitcast.49), channel_id=1, source_target_pairs={{0,2},{1,3},{2,0},{3,1},{4,6},{5,7},{6,4},{7,5},{8,10},{9,11},{10,... | collective-permute-start | bytes 737288 | tf_op jit(solution)/shard_map/gather_w_out/ppermute | solution.py:423
  10.6 1.3 copy-start.1
  11.9 0.7 copy-start.3
  12.6 0.7 copy-start.4
  18.5 19.4 %collective-permute-start.1 = (bf16[64,5120]{1,0:T(8,128)(2,1)}, bf16[64,5120]{1,0:T(8,128)(2,1)}, u32[]{:S(2)}, u32[]{:S(2)}) collective-permute-start(bf16[64,5120]{1,0:T(8,128)(2,1)} %get-tuple-element.34.refs_0_), channel_id=1, source_target_pairs={{0,1},{1,2},{2,3},{3,0},{4,5},{5,6},{6,7},{7,4},{8,9},{9,10},{10,1... | collective-permute-start | bytes 1966088 | tf_op jit(solution)/shard_map/qkv/ppermute | solution.py:423
  19.9 18.1 %collective-permute-start.2 = (bf16[64,5120]{1,0:T(8,128)(2,1)S(1)}, bf16[64,5120]{1,0:T(8,128)(2,1)}, u32[]{:S(2)}, u32[]{:S(2)}) collective-permute-start(bf16[64,5120]{1,0:T(8,128)(2,1)S(1)} %get-tuple-element.35.refs_1_), channel_id=1, source_target_pairs={{0,3},{1,0},{2,1},{3,2},{4,7},{5,4},{6,5},{7,6},{8,11},{9,8},{10,9... | collective-permute-start | bytes 1966088 | tf_op jit(solution)/shard_map/qkv/ppermute | solution.py:423
  22.1 29.6 %collective-permute-start.5 = (bf16[64,5120]{1,0:T(8,128)(2,1)}, bf16[64,5120]{1,0:T(8,128)(2,1)}, u32[]{:S(2)}, u32[]{:S(2)}) collective-permute-start(bf16[64,5120]{1,0:T(8,128)(2,1)} %get-tuple-element.34.refs_0_), channel_id=1, source_target_pairs={{0,3},{1,0},{2,1},{3,2},{4,7},{5,4},{6,5},{7,6},{8,11},{9,8},{10,9... | collective-permute-start | bytes 1966088 | tf_op jit(solution)/shard_map/qkv/ppermute | solution.py:423
  24.0 28.0 %collective-permute-start.6 = (bf16[64,5120]{1,0:T(8,128)(2,1)S(1)}, bf16[64,5120]{1,0:T(8,128)(2,1)}, u32[]{:S(2)}, u32[]{:S(2)}) collective-permute-start(bf16[64,5120]{1,0:T(8,128)(2,1)S(1)} %get-tuple-element.35.refs_1_), channel_id=1, source_target_pairs={{0,1},{1,2},{2,3},{3,0},{4,5},{5,6},{6,7},{7,4},{8,9},{9,10},{10,1... | collective-permute-start | bytes 1966088 | tf_op jit(solution)/shard_map/qkv/ppermute | solution.py:423
  38.0 28.4 %collective-permute-start.3 = (bf16[64,5120]{1,0:T(8,128)(2,1)}, bf16[64,5120]{1,0:T(8,128)(2,1)S(1)}, u32[]{:S(2)}, u32[]{:S(2)}) collective-permute-start(bf16[64,5120]{1,0:T(8,128)(2,1)} %collective-permute-done.1.refs_2_), channel_id=1, source_target_pairs={{0,1},{1,2},{2,3},{3,0},{4,5},{5,6},{6,7},{7,4},{8,9},{9,10},{10,1... | collective-permute-start | bytes 1966088 | tf_op jit(solution)/shard_map/qkv/ppermute | solution.py:423
  39.6 26.8 %collective-permute-start.4 = (bf16[64,5120]{1,0:T(8,128)(2,1)}, bf16[64,5120]{1,0:T(8,128)(2,1)S(1)}, u32[]{:S(2)}, u32[]{:S(2)}) collective-permute-start(bf16[64,5120]{1,0:T(8,128)(2,1)} %collective-permute-done.2.refs_1_), channel_id=1, source_target_pairs={{0,3},{1,0},{2,1},{3,2},{4,7},{5,4},{6,5},{7,6},{8,11},{9,8},{10,9... | collective-permute-start | bytes 1966088 | tf_op jit(solution)/shard_map/qkv/ppermute | solution.py:423
  73.5 7.2 %copy-start.5 = (s32[3,32,4,4]{1,3,2,0:T(4,128)S(1)}, s32[3,32,4,4]{1,3,2,0:T(4,128)}, u32[]{:S(2)}) copy-start(s32[3,32,4,4]{1,3,2,0:T(4,128)} %param.21) | copy-start | bytes 18436
  73.5 7.3 %copy-start.9 = (s32[4]{0:T(128)S(1)}, s32[4]{0:T(128)}, u32[]{:S(2)}) copy-start(s32[4]{0:T(128)} %constant.152.clone) | copy-start | bytes 52
  73.5 10.0 %copy-start.8 = (s32[4]{0:T(128)S(1)}, s32[4]{0:T(128)}, u32[]{:S(2)}) copy-start(s32[4]{0:T(128)} %param.22) | copy-start | bytes 52
  73.5 34.9 %all-to-all-start = ((bf16[16,128,384]{2,1,0:T(8,128)(2,1)}), bf16[16,128,384]{2,1,0:T(8,128)(2,1)}, u32[]{:S(2)}, u32[]{:S(2)}) async-start(bf16[16,128,384]{2,1,0:T(8,128)(2,1)} %bitcast.8), calls=%async_computation | async-start | bytes 3145728 | tf_op jit(solution)/shard_map/spatial/all_to_all | solution.py:488
  92.7 8.3 %collective-permute-start.7 = (bf16[3,3,128,128]{3,2,1,0:T(8,128)(2,1)S(1)}, bf16[3,3,128,128]{3,2,1,0:T(8,128)(2,1)S(1)}, u32[]{:S(2)}, u32[]{:S(2)}) collective-permute-start(bf16[3,3,128,128]{3,2,1,0:T(8,128)(2,1)S(1)} %slice.24), channel_id=1, source_target_pairs={{0,2},{1,3},{2,0},{3,1},{4,6},{5,7},{6,4},{7,5},{8,10},{9,11},{10,... | collective-permute-start | bytes 884744 | tf_op jit(solution)/shard_map/temporal/ppermute | solution.py:423
  108.4 7.7 %collective-permute-start.8 = (bf16[16,128,384]{2,1,0:T(8,128)(2,1)}, bf16[16,128,384]{2,1,0:T(8,128)(2,1)S(1)}, u32[]{:S(2)}, u32[]{:S(2)}) collective-permute-start(bf16[16,128,384]{2,1,0:T(8,128)(2,1)} %all-to-all-done.refs_0_.refs_1_), channel_id=1, source_target_pairs={{0,4},{4,0},{1,5},{5,1},{2,6},{6,2},{3,7},{7,3},{8,12},{12,8},{9,1... | collective-permute-start | bytes 4718600 | tf_op jit(solution)/shard_map/spatial/ppermute | solution.py:426
  116.1 32.0 %slice-start = ((s8[15728640]{0:T(1024)(128)(4,1)}), s8[4194304]{0:T(1024)(128)(4,1)S(1)}, s32[]{:S(2)}) async-start(s8[15728640]{0:T(1024)(128)(4,1)} %bitcast.33), calls=%async_computation.3 | async-start | bytes 8388608
  116.1 32.0 %slice-start.1 = ((s8[15728640]{0:T(1024)(128)(4,1)}), s8[4194304]{0:T(1024)(128)(4,1)S(1)}, s32[]{:S(2)}) async-start(s8[15728640]{0:T(1024)(128)(4,1)} %bitcast.33), calls=%async_computation.4 | async-start | bytes 8388608
  138.5 9.6 %slice-start.2 = ((s8[15728640]{0:T(1024)(128)(4,1)}), s8[4194304]{0:T(1024)(128)(4,1)S(1)}, s32[]{:S(2)}) async-start(s8[15728640]{0:T(1024)(128)(4,1)} %bitcast.33), calls=%async_computation.5 | async-start | bytes 8388608
  138.6 9.6 %slice-start.3 = ((s8[15728640]{0:T(1024)(128)(4,1)}), s8[3145728]{0:T(1024)(128)(4,1)S(1)}, s32[]{:S(2)}) async-start(s8[15728640]{0:T(1024)(128)(4,1)} %bitcast.33), calls=%async_computation.6 | async-start | bytes 6291456
  138.6 9.6 %collective-permute-start.9 = (bf16[3,3,128,128]{3,2,1,0:T(8,128)(2,1)S(1)}, bf16[3,3,128,128]{3,2,1,0:T(8,128)(2,1)S(1)}, u32[]{:S(2)}, u32[]{:S(2)}) collective-permute-start(bf16[3,3,128,128]{3,2,1,0:T(8,128)(2,1)S(1)} %slice.25), channel_id=1, source_target_pairs={{0,2},{1,3},{2,0},{3,1},{4,6},{5,7},{6,4},{7,5},{8,10},{9,11},{10,... | collective-permute-start | bytes 884744 | tf_op jit(solution)/shard_map/spatial/ppermute | solution.py:423
  151.8 16.3 %collective-permute-start.10 = (bf16[128,2560]{1,0:T(8,128)(2,1)S(1)}, bf16[128,2560]{1,0:T(8,128)(2,1)S(1)}, u32[]{:S(2)}, u32[]{:S(2)}) collective-permute-start(bf16[128,2560]{1,0:T(8,128)(2,1)S(1)} %get-tuple-element.57), channel_id=1, source_target_pairs={{0,1},{1,2},{2,3},{3,0},{4,5},{5,6},{6,7},{7,4},{8,9},{9,10},{10,1... | collective-permute-start | bytes 1966088 | tf_op jit(solution)/shard_map/project/ppermute | solution.py:423
  153.5 14.6 %copy-start.2 = (f32[5120]{0:T(1024)S(1)}, f32[5120]{0:T(1024)}, u32[]{:S(2)}) copy-start(f32[5120]{0:T(1024)} %param.16) | copy-start | bytes 61444
  153.5 14.6 %collective-permute-start.11 = (bf16[128,2560]{1,0:T(8,128)(2,1)S(1)}, bf16[128,2560]{1,0:T(8,128)(2,1)S(1)}, u32[]{:S(2)}, u32[]{:S(2)}) collective-permute-start(bf16[128,2560]{1,0:T(8,128)(2,1)S(1)} %get-tuple-element.58), channel_id=1, source_target_pairs={{0,3},{1,0},{2,1},{3,2},{4,7},{5,4},{6,5},{7,6},{8,11},{9,8},{10,9... | collective-permute-start | bytes 1966088 | tf_op jit(solution)/shard_map/project/ppermute | solution.py:423
Sparse Core Ops, SparseCore 0:
  18.7 87.2 all-gather.2
